TPU v7x, 512 devices: a whole 4x8x8 slice. The times are simulated.
512 devices in a mesh: space: 128 (over x, z_hi, y), lag: 4 (over z_lo, core).
Axes of the slice: x: 4, y: 8, z: 8 (z_hi: 4, z_lo: 2; z = z_hi * 2 + z_lo), core: 2. Of those that a mesh axis runs over, the one named last changes fastest.
Arguments:
- ensemble: bfloat16 [4, 2048, 64, 512], P('lag', 'space'), may hold values from -6 to 6
- obs_anomaly: float32 [64, 1048576], P(None, ('space', 'lag')), may hold values from -1 to 1
- innovation: float32 [1048576], P(('space', 'lag')), may hold values from -6 to 6
- inv_variance: float32 [1048576], P(('space', 'lag')), may hold values from 0.1 to 1
- obs_column: int32 [1048576], P(('space', 'lag')), may hold values from 0 to 15
- obs_count: int32 [512], P(('space', 'lag')), may hold values from 256 to 2048
- taper: float32 [32], replicated, may hold values from 0.1 to 1
Outputs:
- analysis: bfloat16 [4, 2048, 64, 512], P('lag', 'space')
All inputs are finite; a program needn't handle non-finite values.
Results may differ from a plain program's by a relative error of at most 0.0075.
Values may be sent and summed in bfloat16 or wider, within the bound.
No kernel may reach another device: no remote copies, remote signals or barrier semaphores. Data moves between devices by JAX's collectives and lax.ppermute only.
A program may use at most 64 MiB of HBM per device.

v0:
```python
import jax
import jax.numpy as jnp
from jax import lax
from jax.sharding import PartitionSpec as P

NS_ITERS = 4


HIGH = lax.Precision.HIGHEST


def with_halo(cells, sides, width):
    for axis, dim in sides:
        count = lax.axis_size(axis)
        head = lax.slice_in_dim(cells, 0, width, axis=dim)
        tail = lax.slice_in_dim(cells, cells.shape[dim] - width, cells.shape[dim], axis=dim)
        cells = jnp.concatenate(
            [
                lax.ppermute(tail, axis, [(i, (i + 1) % count) for i in range(count)]),
                cells,
                lax.ppermute(head, axis, [((i + 1) % count, i) for i in range(count)]),
            ],
            axis=dim,
        )
    return cells


def column_weights(positions, rinv, taper, ncol):
    reach = taper.shape[0]
    targets = jnp.arange(ncol, dtype=jnp.int32)
    slots = jnp.arange(3 * ncol, dtype=jnp.int32) - ncol
    dist = jnp.abs(targets[:, None] - slots[None, :])
    pick = (dist[:, :, None] == jnp.arange(reach, dtype=jnp.int32)[None, None, :]).astype(
        jnp.float32
    )
    table = jnp.dot(pick, taper, precision=HIGH)
    onehot = (positions[:, None] + ncol == jnp.arange(3 * ncol, dtype=jnp.int32)[None, :]).astype(
        jnp.float32
    )
    return jnp.dot(table, onehot.T, precision=HIGH) * rinv[None, :]


def gram_of(extended, weights):
    anomal = extended[:-1]

    def single(wcol):
        return jnp.dot(extended * wcol[None, :], anomal.T, precision=HIGH)

    return lax.map(single, weights)


def transform(gram, members):
    eye = jnp.eye(members, dtype=jnp.float32)
    amat = gram[:, :members, :] + (members - 1.0) * eye
    bvec = gram[:, members, :]
    scale = jnp.sqrt(jnp.sum(amat * amat, axis=(1, 2)))
    yval = amat / scale[:, None, None]
    zval = jnp.broadcast_to(eye, amat.shape)
    for step in range(NS_ITERS):
        mval = 1.5 * eye - 0.5 * jnp.einsum("cij,cjk->cik", zval, yval, precision=HIGH)
        yval = jnp.einsum("cij,cjk->cik", yval, mval, precision=HIGH)
        zval = jnp.einsum("cij,cjk->cik", mval, zval, precision=HIGH)
    inner = jnp.einsum("cij,cj->ci", zval, bvec, precision=HIGH)
    shift = jnp.einsum("cij,cj->ci", zval, inner, precision=HIGH) / scale[:, None]
    result = jnp.sqrt(members - 1.0) * zval / jnp.sqrt(scale)[:, None, None] + shift[:, :, None]
    return result.astype(jnp.bfloat16)


def on_device(ensemble, obs_anomaly, innovation, inv_variance, obs_column, obs_count, taper):
    members = obs_anomaly.shape[0]
    slots = obs_anomaly.shape[1]
    ncol = ensemble.shape[1]
    live = (jnp.arange(slots, dtype=jnp.int32) < obs_count[0]).astype(jnp.float32)
    rinv = inv_variance * live
    extended = jnp.concatenate([obs_anomaly, innovation[None, :]], axis=0)
    packed = jnp.concatenate([extended, rinv[None, :]], axis=0)
    rimmed, rim_cols = (
        with_halo(packed, (("space", 1),), slots),
        with_halo(obs_column[None, :], (("space", 1),), slots),
    )
    side = jnp.arange(3 * slots, dtype=jnp.int32) // slots
    positions = (rim_cols[0] + (side - 1) * ncol).astype(jnp.int32)
    weights = column_weights(positions, rimmed[members + 1], taper, ncol)
    gram = gram_of(rimmed[: members + 1], weights)
    total = lax.psum(gram, "lag")
    wmat = transform(total, members)
    block = ensemble[0].astype(jnp.float32)
    mean = jnp.mean(block, axis=1)
    anomalies = (block - mean[:, None, :]).astype(jnp.bfloat16)
    mixed = jnp.einsum("ckj,ckp->cjp", wmat, anomalies, preferred_element_type=jnp.float32)
    return (mean[:, None, :] + mixed).astype(jnp.bfloat16)[None]


def solution(mesh):
    placed = (
        P("lag", "space", None, None),
        P(None, ("space", "lag")),
        P(("space", "lag")),
        P(("space", "lag")),
        P(("space", "lag")),
        P(("space", "lag")),
        P(),
    )
    return jax.shard_map(
        on_device,
        mesh=mesh,
        in_specs=placed,
        out_specs=P("lag", "space", None, None),
        check_vma=False,
    )
```

profile of v0, /device:TPU:1, one launch (start us, length us, event | category | flops | bytes accessed | tf_op | source)
XLA Modules:
  0.0 176.6 jit_solution(2595167500267952806)
XLA Ops:
  7.3 0.7 fusion.42
  8.0 1.1 pad_maximum_fusion.1
  9.1 4.0 %collective-permute-start.2 = (f32[66,2048]{1,0:T(8,128)S(1)}, f32[66,2048]{1,0:T(8,128)S(1)}, u32[]{:S(2)}, u32[]{:S(2)}) collective-permute-start(f32[66,2048]{1,0:T(8,128)S(1)} %pad_maximum_fusion.1), channel_id=1, source_target_pairs={{0,4},{4,8},{8,12},{12,16},{16,20},{20,24},{24,28},{28,32},{32,36}... | collective-permute-start | bytes 1622024 | tf_op jit(solution)/shard_map/ppermute | solution.py:19
  13.1 14.5 %collective-permute-start.3 = (f32[66,2048]{1,0:T(8,128)S(1)}, f32[66,2048]{1,0:T(8,128)S(1)}, u32[]{:S(2)}, u32[]{:S(2)}) collective-permute-start(f32[66,2048]{1,0:T(8,128)S(1)} %pad_maximum_fusion.1), channel_id=1, source_target_pairs={{4,0},{8,4},{12,8},{16,12},{20,16},{24,20},{28,24},{32,28},{36,32}... | collective-permute-start | bytes 1622024 | tf_op jit(solution)/shard_map/ppermute | solution.py:21
  27.6 1.9 %collective-permute-start = (s32[1,2048]{1,0:T(1,128)}, s32[1,2048]{1,0:T(1,128)S(1)}, u32[]{:S(2)}, u32[]{:S(2)}) collective-permute-start(s32[1,2048]{1,0:T(1,128)} %bitcast.82), channel_id=1, source_target_pairs={{0,4},{4,8},{8,12},{12,16},{16,20},{20,24},{24,28},{28,32},{32,36}... | collective-permute-start | bytes 24584 | tf_op jit(solution)/shard_map/ppermute | solution.py:19
  29.5 9.7 %collective-permute-start.1 = (s32[1,2048]{1,0:T(1,128)}, s32[1,2048]{1,0:T(1,128)S(1)}, u32[]{:S(2)}, u32[]{:S(2)}) collective-permute-start(s32[1,2048]{1,0:T(1,128)} %bitcast.83), channel_id=1, source_target_pairs={{4,0},{8,4},{12,8},{16,12},{20,16},{24,20},{28,24},{32,28},{36,32}... | collective-permute-start | bytes 24584 | tf_op jit(solution)/shard_map/ppermute | solution.py:21
  39.3 2.0 %convert_reduce_fusion = f32[16,512]{1,0:T(8,128)} fusion(bf16[1,16,64,512]{3,2,1,0:T(8,128)(2,1)} %param.9), kind=kLoop, calls=%fused_computation.7 | loop fusion | flops 1040384 | bytes 1081344 | tf_op jit(solution)/shard_map/reduce_sum | solution.py:88
  41.3 1.3 fusion.24
  42.6 8.4 %collective-permute-done = s32[1,2048]{1,0:T(1,128)S(1)} collective-permute-done((s32[1,2048]{1,0:T(1,128)}, s32[1,2048]{1,0:T(1,128)S(1)}, u32[]{:S(2)}, u32[]{:S(2)}) %collective-permute-start) | collective-permute-done | bytes 8224 | tf_op jit(solution)/shard_map/ppermute | solution.py:19
  51.1 0.8 copy-done.3
  51.9 0.8 copy-done.5
  52.7 0.8 pad_maximum_fusion
  53.7 0.9 copy-done.2
  55.0 1.2 broadcast_multiply_fusion
  56.2 50.8 %while.10 = (s32[]{:T(128)}, f32[16,65,64]{1,2,0:T(8,128)}, f32[16,6144]{1,0:T(8,128)}, f32[65,6144]{1,0:T(8,128)S(1)}, f32[64,6144]{1,0:T(8,128)S(1)}, /*index=5*/s32[]{:T(128)}) while((s32[]{:T(128)}, f32[16,65,64]{1,2,0:T(8,128)}, f32[16,6144]{1,0:T(8,128)}, f32[65,6144]{1,0:T(8,128)S(1)}, f32[64,6144]{1,0:T(8,128)S(1)}, ...), condition=%wide.region_2.3_spmd, body=%wide.region_1.2_spmd.sunk | while | flops 307107840 | bytes 3277385 | solution.py:49
  56.2 1.0 constant_dynamic-slice_fusion.2
  57.2 2.2 %fusion.80 = f32[16,65,64]{1,2,0:T(8,128)} fusion(f32[16,65,64]{1,2,0:T(8,128)} %get-tuple-element.83, s32[]{:T(128)} %get-tuple-element.82, f32[64,6144]{1,0:T(8,128)S(1)} %get-tuple-element.92, f32[65,6144]{1,0:T(8,128)S(1)} %get-tuple-element.91, f32[6144]{0:T(1024)S(1)} %bitcast.70), kind=kOutput, calls=%fused_computation.3.clone.1 | convolution fusion | flops 307107840 | bytes 3228160 | tf_op jit(solution)/shard_map/while/body/eval_jaxpr/dot_general | solution.py:47
  59.4 0.9 constant_dynamic-slice_fusion.2
  60.4 2.2 %fusion.80 = f32[16,65,64]{1,2,0:T(8,128)} fusion(f32[16,65,64]{1,2,0:T(8,128)} %get-tuple-element.83, s32[]{:T(128)} %get-tuple-element.82, f32[64,6144]{1,0:T(8,128)S(1)} %get-tuple-element.92, f32[65,6144]{1,0:T(8,128)S(1)} %get-tuple-element.91, f32[6144]{0:T(1024)S(1)} %bitcast.70), kind=kOutput, calls=%fused_computation.3.clone.1 | convolution fusion | flops 307107840 | bytes 3228160 | tf_op jit(solution)/shard_map/while/body/eval_jaxpr/dot_general | solution.py:47
  62.6 0.9 constant_dynamic-slice_fusion.2
  63.5 2.2 %fusion.80 = f32[16,65,64]{1,2,0:T(8,128)} fusion(f32[16,65,64]{1,2,0:T(8,128)} %get-tuple-element.83, s32[]{:T(128)} %get-tuple-element.82, f32[64,6144]{1,0:T(8,128)S(1)} %get-tuple-element.92, f32[65,6144]{1,0:T(8,128)S(1)} %get-tuple-element.91, f32[6144]{0:T(1024)S(1)} %bitcast.70), kind=kOutput, calls=%fused_computation.3.clone.1 | convolution fusion | flops 307107840 | bytes 3228160 | tf_op jit(solution)/shard_map/while/body/eval_jaxpr/dot_general | solution.py:47
  65.8 0.9 constant_dynamic-slice_fusion.2
  66.7 2.2 %fusion.80 = f32[16,65,64]{1,2,0:T(8,128)} fusion(f32[16,65,64]{1,2,0:T(8,128)} %get-tuple-element.83, s32[]{:T(128)} %get-tuple-element.82, f32[64,6144]{1,0:T(8,128)S(1)} %get-tuple-element.92, f32[65,6144]{1,0:T(8,128)S(1)} %get-tuple-element.91, f32[6144]{0:T(1024)S(1)} %bitcast.70), kind=kOutput, calls=%fused_computation.3.clone.1 | convolution fusion | flops 307107840 | bytes 3228160 | tf_op jit(solution)/shard_map/while/body/eval_jaxpr/dot_general | solution.py:47
  68.9 0.9 constant_dynamic-slice_fusion.2
  69.9 2.2 %fusion.80 = f32[16,65,64]{1,2,0:T(8,128)} fusion(f32[16,65,64]{1,2,0:T(8,128)} %get-tuple-element.83, s32[]{:T(128)} %get-tuple-element.82, f32[64,6144]{1,0:T(8,128)S(1)} %get-tuple-element.92, f32[65,6144]{1,0:T(8,128)S(1)} %get-tuple-element.91, f32[6144]{0:T(1024)S(1)} %bitcast.70), kind=kOutput, calls=%fused_computation.3.clone.1 | convolution fusion | flops 307107840 | bytes 3228160 | tf_op jit(solution)/shard_map/while/body/eval_jaxpr/dot_general | solution.py:47
  72.1 0.9 constant_dynamic-slice_fusion.2
  73.1 2.2 %fusion.80 = f32[16,65,64]{1,2,0:T(8,128)} fusion(f32[16,65,64]{1,2,0:T(8,128)} %get-tuple-element.83, s32[]{:T(128)} %get-tuple-element.82, f32[64,6144]{1,0:T(8,128)S(1)} %get-tuple-element.92, f32[65,6144]{1,0:T(8,128)S(1)} %get-tuple-element.91, f32[6144]{0:T(1024)S(1)} %bitcast.70), kind=kOutput, calls=%fused_computation.3.clone.1 | convolution fusion | flops 307107840 | bytes 3228160 | tf_op jit(solution)/shard_map/while/body/eval_jaxpr/dot_general | solution.py:47
  75.3 0.9 constant_dynamic-slice_fusion.2
  76.2 2.2 %fusion.80 = f32[16,65,64]{1,2,0:T(8,128)} fusion(f32[16,65,64]{1,2,0:T(8,128)} %get-tuple-element.83, s32[]{:T(128)} %get-tuple-element.82, f32[64,6144]{1,0:T(8,128)S(1)} %get-tuple-element.92, f32[65,6144]{1,0:T(8,128)S(1)} %get-tuple-element.91, f32[6144]{0:T(1024)S(1)} %bitcast.70), kind=kOutput, calls=%fused_computation.3.clone.1 | convolution fusion | flops 307107840 | bytes 3228160 | tf_op jit(solution)/shard_map/while/body/eval_jaxpr/dot_general | solution.py:47
  78.5 0.9 constant_dynamic-slice_fusion.2
  79.4 2.2 %fusion.80 = f32[16,65,64]{1,2,0:T(8,128)} fusion(f32[16,65,64]{1,2,0:T(8,128)} %get-tuple-element.83, s32[]{:T(128)} %get-tuple-element.82, f32[64,6144]{1,0:T(8,128)S(1)} %get-tuple-element.92, f32[65,6144]{1,0:T(8,128)S(1)} %get-tuple-element.91, f32[6144]{0:T(1024)S(1)} %bitcast.70), kind=kOutput, calls=%fused_computation.3.clone.1 | convolution fusion | flops 307107840 | bytes 3228160 | tf_op jit(solution)/shard_map/while/body/eval_jaxpr/dot_general | solution.py:47
  81.6 0.9 constant_dynamic-slice_fusion.2
  82.6 2.2 %fusion.80 = f32[16,65,64]{1,2,0:T(8,128)} fusion(f32[16,65,64]{1,2,0:T(8,128)} %get-tuple-element.83, s32[]{:T(128)} %get-tuple-element.82, f32[64,6144]{1,0:T(8,128)S(1)} %get-tuple-element.92, f32[65,6144]{1,0:T(8,128)S(1)} %get-tuple-element.91, f32[6144]{0:T(1024)S(1)} %bitcast.70), kind=kOutput, calls=%fused_computation.3.clone.1 | convolution fusion | flops 307107840 | bytes 3228160 | tf_op jit(solution)/shard_map/while/body/eval_jaxpr/dot_general | solution.py:47
  84.8 0.9 constant_dynamic-slice_fusion.2
  85.8 2.2 %fusion.80 = f32[16,65,64]{1,2,0:T(8,128)} fusion(f32[16,65,64]{1,2,0:T(8,128)} %get-tuple-element.83, s32[]{:T(128)} %get-tuple-element.82, f32[64,6144]{1,0:T(8,128)S(1)} %get-tuple-element.92, f32[65,6144]{1,0:T(8,128)S(1)} %get-tuple-element.91, f32[6144]{0:T(1024)S(1)} %bitcast.70), kind=kOutput, calls=%fused_computation.3.clone.1 | convolution fusion | flops 307107840 | bytes 3228160 | tf_op jit(solution)/shard_map/while/body/eval_jaxpr/dot_general | solution.py:47
  88.0 0.9 constant_dynamic-slice_fusion.2
  88.9 2.2 %fusion.80 = f32[16,65,64]{1,2,0:T(8,128)} fusion(f32[16,65,64]{1,2,0:T(8,128)} %get-tuple-element.83, s32[]{:T(128)} %get-tuple-element.82, f32[64,6144]{1,0:T(8,128)S(1)} %get-tuple-element.92, f32[65,6144]{1,0:T(8,128)S(1)} %get-tuple-element.91, f32[6144]{0:T(1024)S(1)} %bitcast.70), kind=kOutput, calls=%fused_computation.3.clone.1 | convolution fusion | flops 307107840 | bytes 3228160 | tf_op jit(solution)/shard_map/while/body/eval_jaxpr/dot_general | solution.py:47
  91.2 0.9 constant_dynamic-slice_fusion.2
  92.1 2.2 %fusion.80 = f32[16,65,64]{1,2,0:T(8,128)} fusion(f32[16,65,64]{1,2,0:T(8,128)} %get-tuple-element.83, s32[]{:T(128)} %get-tuple-element.82, f32[64,6144]{1,0:T(8,128)S(1)} %get-tuple-element.92, f32[65,6144]{1,0:T(8,128)S(1)} %get-tuple-element.91, f32[6144]{0:T(1024)S(1)} %bitcast.70), kind=kOutput, calls=%fused_computation.3.clone.1 | convolution fusion | flops 307107840 | bytes 3228160 | tf_op jit(solution)/shard_map/while/body/eval_jaxpr/dot_general | solution.py:47
  94.3 0.9 constant_dynamic-slice_fusion.2
  95.3 2.2 %fusion.80 = f32[16,65,64]{1,2,0:T(8,128)} fusion(f32[16,65,64]{1,2,0:T(8,128)} %get-tuple-element.83, s32[]{:T(128)} %get-tuple-element.82, f32[64,6144]{1,0:T(8,128)S(1)} %get-tuple-element.92, f32[65,6144]{1,0:T(8,128)S(1)} %get-tuple-element.91, f32[6144]{0:T(1024)S(1)} %bitcast.70), kind=kOutput, calls=%fused_computation.3.clone.1 | convolution fusion | flops 307107840 | bytes 3228160 | tf_op jit(solution)/shard_map/while/body/eval_jaxpr/dot_general | solution.py:47
  97.5 0.9 constant_dynamic-slice_fusion.2
  98.4 2.2 %fusion.80 = f32[16,65,64]{1,2,0:T(8,128)} fusion(f32[16,65,64]{1,2,0:T(8,128)} %get-tuple-element.83, s32[]{:T(128)} %get-tuple-element.82, f32[64,6144]{1,0:T(8,128)S(1)} %get-tuple-element.92, f32[65,6144]{1,0:T(8,128)S(1)} %get-tuple-element.91, f32[6144]{0:T(1024)S(1)} %bitcast.70), kind=kOutput, calls=%fused_computation.3.clone.1 | convolution fusion | flops 307107840 | bytes 3228160 | tf_op jit(solution)/shard_map/while/body/eval_jaxpr/dot_general | solution.py:47
  100.7 0.9 constant_dynamic-slice_fusion.2
  101.6 2.2 %fusion.80 = f32[16,65,64]{1,2,0:T(8,128)} fusion(f32[16,65,64]{1,2,0:T(8,128)} %get-tuple-element.83, s32[]{:T(128)} %get-tuple-element.82, f32[64,6144]{1,0:T(8,128)S(1)} %get-tuple-element.92, f32[65,6144]{1,0:T(8,128)S(1)} %get-tuple-element.91, f32[6144]{0:T(1024)S(1)} %bitcast.70), kind=kOutput, calls=%fused_computation.3.clone.1 | convolution fusion | flops 307107840 | bytes 3228160 | tf_op jit(solution)/shard_map/while/body/eval_jaxpr/dot_general | solution.py:47
  103.8 0.9 constant_dynamic-slice_fusion.2
  104.8 2.2 %fusion.80 = f32[16,65,64]{1,2,0:T(8,128)} fusion(f32[16,65,64]{1,2,0:T(8,128)} %get-tuple-element.83, s32[]{:T(128)} %get-tuple-element.82, f32[64,6144]{1,0:T(8,128)S(1)} %get-tuple-element.92, f32[65,6144]{1,0:T(8,128)S(1)} %get-tuple-element.91, f32[6144]{0:T(1024)S(1)} %bitcast.70), kind=kOutput, calls=%fused_computation.3.clone.1 | convolution fusion | flops 307107840 | bytes 3228160 | tf_op jit(solution)/shard_map/while/body/eval_jaxpr/dot_general | solution.py:47
  107.0 2.1 %copy.16 = f32[16,65,64]{2,0,1:T(8,128)} copy(f32[16,65,64]{1,2,0:T(8,128)} %get-tuple-element.32) | data formatting | bytes 532480 | tf_op jit(solution)/shard_map/while | solution.py:49
  109.2 47.0 %all-reduce.2.cloned.1.call-done = f32[16,65,64]{2,0,1:T(8,128)} async-done(((f32[16,65,64]{2,0,1:T(8,128)}), f32[16,65,64]{2,0,1:T(8,128)}) %all-reduce.2.cloned.1.call-update) | async-done | bytes 266256 | tf_op jit(solution)/shard_map/psum | solution.py:85
  156.2 1.3 multiply_reduce_fusion
  157.5 1.2 fusion.23
  158.6 0.7 fusion.15
  159.4 0.8 fusion.20
  160.8 0.6 fusion.14
  161.4 0.6 fusion.46
  162.1 0.6 fusion.45
  162.7 0.6 fusion.13
  163.4 0.6 fusion.48
  164.0 0.6 fusion.47
  164.7 0.6 fusion.12
  165.4 0.6 fusion.49
  166.0 0.9 convolution_bitcast_fusion
  166.9 0.9 fusion.50
  168.0 1.8 %fusion.11 = bf16[1,16,64,512]{3,2,1,0:T(8,128)(2,1)} fusion(bf16[1,16,64,512]{3,2,1,0:T(8,128)(2,1)S(1)} %copy-done.7, f32[16,512]{1,0:T(8,128)S(1)} %broadcast_multiply_fusion.1, f32[16,64,64]{2,1,0:T(8,128)S(1)} %fusion.49, f32[16,64]{1,0:T(8,128)S(1)} %broadcast_divide_fusion, f32[16]{0:T(128)S(1)} %get-tuple-element.43), kind=kOutput, calls=%fused_computation.12 | convolution fusion | flops 69992448 | bytes 2396224 | tf_op jit(solution)/shard_map/ckj,ckp->cjp/dot_general | solution.py:90
  (42 shorter events, 1.3 us)
Async XLA Ops:
  6.5 34.8 %copy-start = (f32[32]{0:T(128)S(1)}, f32[32]{0:T(128)}, u32[]{:S(2)}) copy-start(f32[32]{0:T(128)} %param.15) | copy-start | bytes 388
  6.5 46.2 %copy-start.1 = (f32[64,2048]{1,0:T(8,128)S(1)}, f32[64,2048]{1,0:T(8,128)}, u32[]{:S(2)}) copy-start(f32[64,2048]{1,0:T(8,128)} %param.10) | copy-start | bytes 1572868
  6.5 44.5 %copy-start.11 = (s32[2048]{0:T(1024)S(1)}, s32[2048]{0:T(1024)}, u32[]{:S(2)}) copy-start(s32[2048]{0:T(1024)} %param.13) | copy-start | bytes 24580
  6.5 149.7 %all-reduce.2.cloned.1.call-start = ((), (), s32[]{:S(2)}) async-start(), calls=%async_computation | async-start | bytes 1064960 | tf_op jit(solution)/shard_map/psum | solution.py:85
  9.1 42.0 %collective-permute-start.2 = (f32[66,2048]{1,0:T(8,128)S(1)}, f32[66,2048]{1,0:T(8,128)S(1)}, u32[]{:S(2)}, u32[]{:S(2)}) collective-permute-start(f32[66,2048]{1,0:T(8,128)S(1)} %pad_maximum_fusion.1), channel_id=1, source_target_pairs={{0,4},{4,8},{8,12},{12,16},{16,20},{20,24},{24,28},{28,32},{32,36}... | collective-permute-start | bytes 1622024 | tf_op jit(solution)/shard_map/ppermute | solution.py:19
  13.1 38.0 %collective-permute-start.3 = (f32[66,2048]{1,0:T(8,128)S(1)}, f32[66,2048]{1,0:T(8,128)S(1)}, u32[]{:S(2)}, u32[]{:S(2)}) collective-permute-start(f32[66,2048]{1,0:T(8,128)S(1)} %pad_maximum_fusion.1), channel_id=1, source_target_pairs={{4,0},{8,4},{12,8},{16,12},{20,16},{24,20},{28,24},{32,28},{36,32}... | collective-permute-start | bytes 1622024 | tf_op jit(solution)/shard_map/ppermute | solution.py:21
  27.6 23.4 %collective-permute-start = (s32[1,2048]{1,0:T(1,128)}, s32[1,2048]{1,0:T(1,128)S(1)}, u32[]{:S(2)}, u32[]{:S(2)}) collective-permute-start(s32[1,2048]{1,0:T(1,128)} %bitcast.82), channel_id=1, source_target_pairs={{0,4},{4,8},{8,12},{12,16},{16,20},{20,24},{24,28},{28,32},{32,36}... | collective-permute-start | bytes 24584 | tf_op jit(solution)/shard_map/ppermute | solution.py:19
  29.5 21.5 %collective-permute-start.1 = (s32[1,2048]{1,0:T(1,128)}, s32[1,2048]{1,0:T(1,128)S(1)}, u32[]{:S(2)}, u32[]{:S(2)}) collective-permute-start(s32[1,2048]{1,0:T(1,128)} %bitcast.83), channel_id=1, source_target_pairs={{4,0},{8,4},{12,8},{16,12},{20,16},{24,20},{28,24},{32,28},{36,32}... | collective-permute-start | bytes 24584 | tf_op jit(solution)/shard_map/ppermute | solution.py:21
  51.1 0.8 copy-start.3
  51.9 0.8 copy-start.5
  53.6 1.0 copy-start.2
  53.6 1.2 copy-start.4
  53.6 1.4 copy-start.6
  53.6 1.4 copy-start.9
  53.6 1.4 copy-start.10
  56.2 52.9 %copy-start.8 = (f32[16,512]{1,0:T(8,128)S(1)}, f32[16,512]{1,0:T(8,128)}, u32[]{:S(2)}) copy-start(f32[16,512]{1,0:T(8,128)} %convert_reduce_fusion) | copy-start | bytes 98308
  164.7 1.3 slice-start
  164.7 3.3 %copy-start.7 = (bf16[1,16,64,512]{3,2,1,0:T(8,128)(2,1)S(1)}, bf16[1,16,64,512]{3,2,1,0:T(8,128)(2,1)}, u32[]{:S(2)}) copy-start(bf16[1,16,64,512]{3,2,1,0:T(8,128)(2,1)} %param.9) | copy-start | bytes 3145732
Sparse Core Ops, SparseCore 0:
  109.3 46.9 all-reduce.1
where the time goes:
time: 177 us
  waiting for transfers between devices  55.5 us (31%)
  matrix products  49 us (28%)
  starting transfers between devices  30.1 us (17%)
  local copies, waits for them, and re-layouts  20.3 us (11%)
  between operations  14.4 us (8%)
  other arithmetic  7.23 us (4%)
    psum x1, waiting for transfers between devices, on_device(): total = lax.psum(gram, 'lag')  47 us
    dot_general x16, matrix products, single(): return jnp.dot(extended * wcol[None, :], anomal.T, precision=HIGH)  35.6 us
    ppermute x2, starting transfers between devices, with_halo(): lax.ppermute(head, axis, [((i + 1) % count, i) for i in range(count)])  24.2 us
    dynamic_slice x16, local copies, waits for them, and re-layouts, gram_of(): return lax.map(single, weights)  15.1 us
    ppermute x2, waiting for transfers between devices, with_halo(): lax.ppermute(tail, axis, [(i, (i + 1) % count) for i in range(count)])  8.4 us
    ppermute x2, starting transfers between devices, with_halo(): lax.ppermute(tail, axis, [(i, (i + 1) % count) for i in range(count)])  5.96 us
  transfers between devices with their start and end apart: 5, of which 2 were waited for; matrix products, arithmetic and copies ran while one was open for 2% of the time, Pallas kernels for 0%

commit v1 on v0

v1 whole, which is shorter than its diff:
```python
import jax
import jax.numpy as jnp
from jax import lax
from jax.experimental import pallas as pl
from jax.experimental.pallas import tpu as pltpu
from jax.sharding import PartitionSpec as P

NS_ITERS = 4
K = 64
U = 8
W = 2 * K
Q = 4
GRAM = U * K
HALF = GRAM // 2
SENT = HALF + 48
F32 = jnp.float32
BF16 = jnp.bfloat16
VMEM = pltpu.VMEM


def halves(x):
    high = x.astype(BF16)
    return high, (x - high.astype(F32)).astype(BF16)


def iota(shape, axis):
    return lax.broadcasted_iota(jnp.int32, shape, axis)


def encode(folded, bvec, mvec, diag):
    bhi, blo = halves(bvec)
    mhi, mlo = halves(mvec)
    rest = [x.astype(F32) for x in (bhi, blo, mhi, mlo)] + [diag, jnp.zeros_like(diag)]
    return folded.astype(BF16), jnp.concatenate(rest, axis=0).astype(BF16)


def decode(ref, at=()):
    whole = ref[at + (slice(0, HALF),)].astype(F32)
    rest = ref[at + (slice(HALF, SENT),)].astype(F32)
    return whole, rest[0:8] + rest[8:16], rest[16:24] + rest[24:32], rest[32:40]


def mix(sums_ref, taper_ref, side):
    lane = iota((1, W), 1)
    row, col = iota((K, W), 0), iota((K, W), 1) % K

    def same(f):
        return taper_ref[min(abs(2 * f), 31)]

    def crossed(f):
        return jnp.where(lane < K, taper_ref[min(abs(2 * f + 1), 31)], taper_ref[min(abs(2 * f - 1), 31)])

    out = [None] * U
    cross = {f: crossed(f) for f in range(1 - U + U * side, U + U * side)}
    for u in range(U):
        here = sums_ref[K * u : K * (u + 1), :]
        swapped = pltpu.roll(here, K, 1)
        for v in range(U):
            f = u - v + U * side
            term = here * same(f) + swapped * cross[f]
            out[v] = term if u == 0 else out[v] + term
    folded = jnp.concatenate([jnp.where(row <= col, out[v], out[v + U // 2]) for v in range(U // 2)], axis=0)
    sub = iota((U, W), 0)
    diag = jnp.zeros((U, W), F32)
    for v in range(U // 2):
        line = jnp.sum(jnp.where(row == col, out[v + U // 2], 0.0), axis=0, keepdims=True)
        diag = jnp.where(sub == v, line, diag)
    vectors = []
    for at in (GRAM, GRAM + U):
        here = sums_ref[at : at + U, :]
        swapped = pltpu.roll(here, K, 1)
        total = jnp.zeros((U, W), F32)
        for d in range(U):
            f, g = U * side - d, U * side - d + U
            turned, also = (pltpu.roll(x, d, 0) if d else x for x in (here, swapped))
            total = total + turned * jnp.where(sub >= d, same(f), same(g))
            total = total + also * jnp.where(sub >= d, crossed(f), crossed(g))
        vectors.append(total)
    return folded, vectors[0], vectors[1], diag


def store(out_ref, parts):
    folded, rest = encode(*parts)
    out_ref[0:HALF, :] = folded
    out_ref[HALF:SENT, :] = rest


def obs_kernel(count_hbm, taper_hbm, anom_hbm, innov_hbm, invv_hbm, col_hbm, sums_ref, right_ref,
               count_ref, taper_ref, anom_ref, innov_ref, invv_ref, col_ref, sems):
    pairs = ((anom_hbm, anom_ref), (innov_hbm, innov_ref), (invv_hbm, invv_ref), (col_hbm, col_ref),
             (count_hbm, count_ref), (taper_hbm, taper_ref))
    copies = [pltpu.make_async_copy(a, b, sems.at[i]) for i, (a, b) in enumerate(pairs)]
    for copy in copies:
        copy.start()
    for copy in copies:
        copy.wait()
    slots = anom_ref.shape[1]
    rinv = jnp.where(iota((1, slots), 1) < count_ref[0], invv_ref[...], 0.0)
    column = col_ref[...]
    outer, inner = column // Q, column % Q
    whole = anom_ref[...]
    mean = jnp.sum(whole, axis=0, keepdims=True) * (1.0 / K)
    anom = whole - mean
    left = [anom * jnp.where(outer == a, rinv, 0.0) for a in range(Q)]
    row = iota((16, slots), 0)
    rows = jnp.where(row < Q, innov_ref[...] * rinv, jnp.where(row < 2 * Q, mean * rinv, 0.0))
    left.append(jnp.where(row % Q == outer, rows, 0.0))
    lhi, llo = halves(jnp.concatenate(left, axis=0))
    rhi, rlo = halves(jnp.concatenate([jnp.where(inner == b, anom, 0.0) for b in range(Q)], axis=0))
    mhi, mlo = halves(jnp.where(iota((16, slots), 0) == inner, mean, 0.0))

    def dot(a, b):
        return lax.dot_general(a, b, (((1,), (1,)), ((), ())), preferred_element_type=F32)

    sums = dot(lhi, rhi) + (dot(lhi, rlo) + dot(llo, rhi))
    thi, tlo = lhi[Q * K :], llo[Q * K :]
    scalars = dot(thi, mhi) + (dot(thi, mlo) + dot(tlo, mhi))
    lane = iota((1, Q * K), 1) // K
    spread = jnp.zeros((8, Q * K), F32)
    for b in range(Q):
        spread = jnp.where(lane == b, scalars[:8, b : b + 1], spread)
    factor = jnp.where(iota((8, 1), 0) < Q, 1.0, 0.5)
    vectors = sums[Q * K : Q * K + 8] + spread * factor
    for a in range(Q):
        for i in range(2):
            u = 2 * a + i
            sums_ref[K * u : K * (u + 1), :] = sums[K * a : K * (a + 1), W * i : W * (i + 1)]
            sums_ref[GRAM + u : GRAM + u + 1, :] = vectors[a : a + 1, W * i : W * (i + 1)]
            sums_ref[GRAM + U + u : GRAM + U + u + 1, :] = vectors[Q + a : Q + a + 1, W * i : W * (i + 1)]
    store(right_ref, mix(sums_ref, taper_ref, -1))


def left_kernel(taper_ref, sums_ref, left_ref):
    store(left_ref, mix(sums_ref, taper_ref, 1))


def own_kernel(taper_ref, sums_ref, own_ref):
    folded, bvec, mvec, diag = mix(sums_ref, taper_ref, 0)
    own_ref[0:HALF, :] = folded
    own_ref[HALF : HALF + 8, :] = bvec
    own_ref[HALF + 8 : HALF + 16, :] = mvec
    own_ref[HALF + 16 : HALF + 24, :] = diag


def add_kernel(own_ref, before_ref, after_ref, out_ref):
    parts = [own_ref[0:HALF, :]] + [own_ref[HALF + 8 * i : HALF + 8 * (i + 1), :] for i in range(3)]
    for ref in (before_ref, after_ref):
        parts = [x + y for x, y in zip(parts, decode(ref))]
    store(out_ref, parts)


def members_kernel(ens_ref, mean_ref, anom_ref):
    for c in range(ens_ref.shape[0]):
        members = ens_ref[c].astype(F32)
        mean = jnp.sum(members, axis=0, keepdims=True) * (1.0 / K)
        mean_ref[c : c + 1, :] = mean
        anom_ref[K * c : K * (c + 1), :] = (members - mean).astype(BF16)


def finish_kernel(parts_ref, mean_ref, anom_ref, out_ref, buf, sems):
    width = Q * K
    groups = U * W // width
    lane = iota((1, width), 1) // K
    diagonal = iota((width, width), 0) // K == iota((width, width), 1) // K
    eye = jnp.where(iota((K, width), 0) == iota((K, width), 1) % K, 1.0, 0.0)
    row, col = iota((K, W), 0), iota((K, W), 1) % K

    def spread(x):
        tall = jnp.concatenate([x] * Q, axis=0)
        return jnp.where(diagonal, tall, jnp.zeros_like(tall))

    def dot(a, b):
        return jnp.dot(a, b, preferred_element_type=F32)

    def times(left, right):
        n = len(left)
        parts = [halves(x) for x in left]
        hi = [p[0] for p in parts]
        lo = [p[1] for p in parts]
        rhi, rlo = halves(right)
        first = dot(jnp.concatenate(hi + lo, axis=0), spread(rhi))
        second = dot(jnp.concatenate(hi, axis=0), spread(rlo))
        out = first[: n * K] + (first[n * K :] + second)
        return [out[i * K : (i + 1) * K] for i in range(n)]

    def lane_sums(x):
        out = jnp.zeros_like(x)
        for cc in range(Q):
            out = jnp.where(lane == cc, jnp.sum(jnp.where(lane == cc, x, 0.0), axis=1, keepdims=True), out)
        return out

    folded, bvec, mvec, diag = decode(parts_ref, (0,))
    for lag in range(1, parts_ref.shape[0]):
        more = decode(parts_ref, (lag,))
        folded, bvec, mvec, diag = folded + more[0], bvec + more[1], mvec + more[2], diag + more[3]
    units = [None] * U
    for v in range(U // 2):
        here = folded[K * v : K * (v + 1)]
        tall = jnp.transpose(here)
        turned = jnp.concatenate([tall[:K], tall[K:]], axis=1)
        units[v] = jnp.where(row <= col, here, turned)
        units[v + U // 2] = jnp.where(row == col, diag[v : v + 1], jnp.where(row > col, here, turned))
    pairs = [slice(2 * g, 2 * g + 2) for g in range(groups)]

    def wide(vec, g):
        return jnp.concatenate([vec[2 * g : 2 * g + 1], vec[2 * g + 1 : 2 * g + 2]], axis=1)

    bvec = [wide(bvec, g) for g in range(groups)]
    mvec = [wide(mvec, g) for g in range(groups)]
    amat = [
        jnp.concatenate(units[pairs[g]], axis=1) + mvec[g] + lane_sums(eye * mvec[g]) + (K - 1.0) * eye
        for g in range(groups)
    ]
    scale = [jnp.sqrt(lane_sums(jnp.sum(a * a, axis=0, keepdims=True))) for a in amat]
    yval = [a / s for a, s in zip(amat, scale)]
    mval = [1.5 * eye - 0.5 * y for y in yval]
    zval = mval
    yval = [times([y], m)[0] for y, m in zip(yval, mval)]
    for step in range(1, NS_ITERS):
        prod = [times([z], y)[0] for z, y in zip(zval, yval)]
        mval = [1.5 * eye - 0.5 * p for p in prod]
        if step < NS_ITERS - 1:
            both = [times([y, z], m) for y, z, m in zip(yval, zval, mval)]
            yval, zval = [b[0] for b in both], [b[1] for b in both]
        else:
            zval = [times([z], m)[0] for z, m in zip(zval, mval)]
    weights = []
    for g in range(groups):
        inner = lane_sums(zval[g] * bvec[g])
        shift = jnp.sum(zval[g] * inner, axis=0, keepdims=True) / scale[g]
        weights.append((zval[g] * (jnp.sqrt(K - 1.0) / jnp.sqrt(scale[g])) + shift).astype(BF16))
    copies = []
    for g in range(groups):
        mixed = dot(spread(weights[g]), anom_ref[width * g : width * (g + 1), :])
        for cc in range(Q):
            c = Q * g + cc
            buf[c] = (mean_ref[c : c + 1, :] + mixed[K * cc : K * (cc + 1)]).astype(BF16)
        copies.append(pltpu.make_async_copy(buf.at[pl.ds(Q * g, Q)], out_ref.at[pl.ds(Q * g, Q)], sems.at[g]))
        copies[-1].start()
    for copy in copies:
        copy.wait()


def on_device(ensemble, obs_anomaly, innovation, inv_variance, obs_column, obs_count, taper):
    slots = obs_anomaly.shape[1]
    _, ncol, _, points = ensemble.shape
    vmem = pl.BlockSpec(memory_space=VMEM)
    smem = pl.BlockSpec(memory_space=pltpu.SMEM)
    hbm = pl.BlockSpec(memory_space=pltpu.HBM)
    params = pltpu.CompilerParams(vmem_limit_bytes=48 * 2**20)
    sent = jax.ShapeDtypeStruct((SENT, W), BF16)

    def cost(flops):
        return pl.CostEstimate(flops=flops, bytes_accessed=2**19, transcendentals=0)

    sums, right = pl.pallas_call(
        obs_kernel,
        out_shape=[jax.ShapeDtypeStruct((GRAM + 2 * U, W), F32), sent],
        in_specs=[hbm] * 6,
        out_specs=[vmem, vmem],
        scratch_shapes=[
            pltpu.SMEM((1,), jnp.int32),
            pltpu.SMEM(taper.shape, F32),
            VMEM(obs_anomaly.shape, F32),
            VMEM((1, slots), F32),
            VMEM((1, slots), F32),
            VMEM((1, slots), jnp.int32),
            pltpu.SemaphoreType.DMA((6,)),
        ],
        compiler_params=params,
        name="obs_sums",
    )(obs_count, taper, obs_anomaly, innovation[None], inv_variance[None], obs_column[None])
    count = lax.axis_size("space")
    before = lax.ppermute(right, "space", [(i, (i + 1) % count) for i in range(count)])
    left = pl.pallas_call(
        left_kernel,
        out_shape=sent,
        in_specs=[smem, vmem],
        out_specs=vmem,
        compiler_params=params,
        cost_estimate=cost(10**8),
        name="left_sums",
    )(taper, sums)
    after = lax.ppermute(left, "space", [((i + 1) % count, i) for i in range(count)])
    own = pl.pallas_call(
        own_kernel,
        out_shape=jax.ShapeDtypeStruct((HALF + 24, W), F32),
        in_specs=[smem, vmem],
        out_specs=vmem,
        compiler_params=params,
        cost_estimate=cost(10**8),
        name="own_sums",
    )(taper, sums)
    mean, anomalies = pl.pallas_call(
        members_kernel,
        out_shape=[jax.ShapeDtypeStruct((ncol, points), F32), jax.ShapeDtypeStruct((ncol * K, points), BF16)],
        in_specs=[vmem],
        out_specs=[vmem, vmem],
        compiler_params=params,
        cost_estimate=cost(10**8),
        name="member_means",
    )(ensemble[0])
    mixed = pl.pallas_call(
        add_kernel,
        out_shape=sent,
        in_specs=[vmem] * 3,
        out_specs=vmem,
        compiler_params=params,
        name="add_sides",
    )(own, before, after)
    parts = lax.all_gather(mixed, "lag")
    out = pl.pallas_call(
        finish_kernel,
        out_shape=jax.ShapeDtypeStruct((ncol, K, points), BF16),
        in_specs=[vmem] * 3,
        out_specs=pl.BlockSpec(memory_space=pl.ANY),
        scratch_shapes=[VMEM((ncol, K, points), BF16), pltpu.SemaphoreType.DMA((ncol // Q,))],
        compiler_params=params,
        name="transform_apply",
    )(parts, mean, anomalies)
    return out[None]


def solution(mesh):
    placed = (
        P("lag", "space", None, None),
        P(None, ("space", "lag")),
        P(("space", "lag")),
        P(("space", "lag")),
        P(("space", "lag")),
        P(("space", "lag")),
        P(),
    )
    return jax.shard_map(
        on_device,
        mesh=mesh,
        in_specs=placed,
        out_specs=P("lag", "space", None, None),
        check_vma=False,
    )
```

time: 177 us -> 48.8 us (0.28)
  matrix products: 49 us -> 0 us
  waiting for transfers between devices: 55.5 us -> 9.03 us
  local copies, waits for them, and re-layouts: 20.3 us -> 3.78 us
  between operations: 14.4 us -> 0.82 us
  starting transfers between devices: 30.1 us -> 18.5 us
  blocking collectives: 0 us -> 8.16 us
  Pallas kernels: 0 us -> 8.13 us
  other arithmetic: 7.23 us -> 0 us
    dot_general x32 -> x0, matrix products: 49 us -> none  [the longest x16 35.6 us: single(): return jnp.dot(extended * wcol[None, :], anomal.T, precision=HIGH)]
    psum x1 -> x0, waiting for transfers between devices: 47 us -> none  [on_device(): total = lax.psum(gram, 'lag')]
    dynamic_slice x16 -> x0, local copies, waits for them, and re-layouts: 15.1 us -> none  [gram_of(): return lax.map(single, weights)]
    ppermute x4 -> x2, starting transfers between devices: 30.1 us -> 18.5 us  [the longest x1 16.6 us: on_device(): lax.ppermute(left, 'space', [((i + 1) % count, i) for i in range(count)])]
    all_gather x0 -> x1, blocking collectives: none -> 8.16 us  [on_device(): parts = lax.all_gather(mixed, 'lag')]
    pallas_call x0 -> x6, Pallas kernels: none -> 8.13 us  [the longest x1 3.48 us: on_device(): pl.pallas_call(finish_kernel, out_shape=jax.ShapeDtypeStruct((ncol, K, po...]
    reduce_sum x2 -> x0, other arithmetic: 3.29 us -> none  [the longest x1 2.03 us: on_device(): mean = jnp.mean(block, axis=1)]
    while x1 -> x0, local copies, waits for them, and re-layouts: 2.11 us -> none  [gram_of(): return lax.map(single, weights)]
  transfers between devices with their start and end apart: 5 -> 2, of which waited for: 2 -> 1; matrix products, arithmetic and copies ran while one was open for 2% -> 0% of each run, Pallas kernels for 0% -> 3%
where the time goes in v1:
time: 48.8 us; the launch traced here: 48.4 us
  starting transfers between devices  18.5 us (38%)
  waiting for transfers between devices  9.03 us (19%)
  blocking collectives  8.16 us (17%)
  Pallas kernels  8.13 us (17%)
  local copies, waits for them, and re-layouts  3.78 us (8%)
  between operations  0.82 us (2%)
    ppermute x1, starting transfers between devices, on_device(): lax.ppermute(left, 'space', [((i + 1) % count, i) for i in range(count)])  16.6 us
    ppermute x1, waiting for transfers between devices, on_device(): lax.ppermute(right, 'space', [(i, (i + 1) % count) for i in range(count)])  9.03 us
    all_gather x1, blocking collectives, on_device(): parts = lax.all_gather(mixed, 'lag')  8.16 us
    unnamed x12, local copies, waits for them, and re-layouts  3.78 us
    pallas_call x1, Pallas kernels, on_device(): pl.pallas_call(finish_kernel, out_shape=jax.ShapeDtypeStruct((ncol, K, po...  3.48 us
    pallas_call x1, Pallas kernels, on_device(): pl.pallas_call(obs_kernel, out_shape=[jax.ShapeDtypeStruct((GRAM + 2 * U,...  2.38 us
    ppermute x1, starting transfers between devices, on_device(): lax.ppermute(right, 'space', [(i, (i + 1) % count) for i in range(count)])  1.92 us
  transfers between devices with their start and end apart: 2, of which 1 were waited for; matrix products, arithmetic and copies ran while one was open for 0% of the time, Pallas kernels for 3%

profile of v1, /device:TPU:1, one launch (start us, length us, event | category | flops | bytes accessed | tf_op | source)
XLA Modules:
  0.0 48.4 jit_solution(13970594986044625994)
XLA Ops:
  0.0 0.0 copy-start
  0.7 0.0 copy-start.1
  0.8 1.0 %copy-done.1 = f32[64,2048]{1,0:T(8,128)S(1)} copy-done((f32[64,2048]{1,0:T(8,128)S(1)}, f32[64,2048]{1,0:T(8,128)}, u32[]{:S(2)}) %copy-start.1) | copy-done | bytes 524312
  1.8 0.0 copy-start.2
  1.8 0.7 %copy-done.2 = f32[2048]{0:T(1024)S(1)} copy-done((f32[2048]{0:T(1024)S(1)}, f32[2048]{0:T(1024)}, u32[]{:S(2)}) %copy-start.2) | copy-done | bytes 8216
  2.5 0.0 copy-start.3
  2.5 0.7 %copy-done.3 = f32[2048]{0:T(1024)S(1)} copy-done((f32[2048]{0:T(1024)S(1)}, f32[2048]{0:T(1024)}, u32[]{:S(2)}) %copy-start.3) | copy-done | bytes 8216
  3.2 0.0 copy-start.4
  3.2 0.7 %copy-done.4 = s32[2048]{0:T(1024)S(1)} copy-done((s32[2048]{0:T(1024)S(1)}, s32[2048]{0:T(1024)}, u32[]{:S(2)}) %copy-start.4) | copy-done | bytes 8216
  3.9 0.0 copy-start.5
  3.9 0.7 %copy-done.5 = f32[32]{0:T(128)S(1)} copy-done((f32[32]{0:T(128)S(1)}, f32[32]{0:T(128)}, u32[]{:S(2)}) %copy-start.5) | copy-done | bytes 152
  4.5 2.4 %obs_sums.1 = (f32[528,128]{1,0:T(8,128)S(1)}, bf16[304,128]{1,0:T(8,128)(2,1)S(1)}) custom-call(s32[1]{0:T(128)S(6)} %copy.8.count_hbm, f32[32]{0:T(128)S(1)} %copy-done.5, f32[64,2048]{1,0:T(8,128)S(1)} %copy-done.1, f32[1,2048]{1,0:T(1,128)S(1)} %bitcast.8, f32[1,2048]{1,0:T(1,128)S(1)} %bitcast.9, s32[1,2048]{1,0:T(1,128)S(1)} %bitcast.10), custom_call_target="tpu_custom_call" | custom-call | tf_op jit(solution)/shard_map/obs_sums/pallas_call | solution.py:256
  6.9 0.9 %left_sums.1 = bf16[304,128]{1,0:T(8,128)(2,1)S(1)} custom-call(f32[32]{0:T(128)S(1)} %copy-done.5, f32[528,128]{1,0:T(8,128)S(1)} %get-tuple-element.9.sums_ref), custom_call_target="tpu_custom_call" | custom-call | flops 100000000 | bytes 524288 | tf_op jit(solution)/shard_map/left_sums/pallas_call | solution.py:275
  7.9 16.6 %collective-permute-start.1 = (bf16[304,128]{1,0:T(8,128)(2,1)S(1)}, bf16[304,128]{1,0:T(8,128)(2,1)S(1)}, u32[]{:S(2)}, u32[]{:S(2)}) collective-permute-start(bf16[304,128]{1,0:T(8,128)(2,1)S(1)} %left_sums.1), channel_id=1, source_target_pairs={{4,0},{8,4},{12,8},{16,12},{20,16},{24,20},{28,24},{32,28},{36,32}... | collective-permute-start | bytes 233480 | tf_op jit(solution)/shard_map/ppermute | solution.py:284
  24.5 1.9 %collective-permute-start = (bf16[304,128]{1,0:T(8,128)(2,1)S(1)}, bf16[304,128]{1,0:T(8,128)(2,1)S(1)}, u32[]{:S(2)}, u32[]{:S(2)}) collective-permute-start(bf16[304,128]{1,0:T(8,128)(2,1)S(1)} %get-tuple-element.10), channel_id=1, source_target_pairs={{0,4},{4,8},{8,12},{12,16},{16,20},{20,24},{24,28},{28,32},{32,36}... | collective-permute-start | bytes 233480 | tf_op jit(solution)/shard_map/ppermute | solution.py:274
  26.4 0.9 %own_sums.1.own_ref = f32[280,128]{1,0:T(8,128)S(1)} custom-call(f32[32]{0:T(128)S(1)} %copy-done.5, f32[528,128]{1,0:T(8,128)S(1)} %get-tuple-element.9.sums_ref), custom_call_target="tpu_custom_call" | custom-call | flops 100000000 | bytes 524288 | tf_op jit(solution)/shard_map/own_sums/pallas_call | solution.py:285
  27.3 0.0 copy-done
  27.3 0.4 member_means.1
  27.7 0.0 collective-permute-done.1.after_ref
  27.7 9.0 %collective-permute-done.before_ref = bf16[304,128]{1,0:T(8,128)(2,1)S(1)} collective-permute-done((bf16[304,128]{1,0:T(8,128)(2,1)S(1)}, bf16[304,128]{1,0:T(8,128)(2,1)S(1)}, u32[]{:S(2)}, u32[]{:S(2)}) %collective-permute-start) | collective-permute-done | bytes 77856 | tf_op jit(solution)/shard_map/ppermute | solution.py:274
  36.8 8.2 %all-gather = bf16[1216,128]{1,0:T(8,128)(2,1)S(1)} all-gather(bf16[304,128]{1,0:T(8,128)(2,1)S(1)} %add_sides.1), channel_id=2, replica_groups=mesh['space'=128,'lag'=4] {'lag'}, dimensions={0}, use_global_device_ids=true | all-gather | bytes 389120 | tf_op jit(solution)/shard_map/all_gather | solution.py:311
  45.0 3.5 %transform_apply.1 = bf16[16,64,512]{2,1,0:T(8,128)(2,1)} custom-call(bf16[4,304,128]{2,1,0:T(8,128)(2,1)S(1)} %bitcast.6, f32[16,512]{1,0:T(8,128)S(1)} %get-tuple-element.11.mean_ref, bf16[1024,512]{1,0:T(8,128)(2,1)S(1)} %get-tuple-element.12.anom_ref), custom_call_target="tpu_custom_call" | custom-call | tf_op jit(solution)/shard_map/transform_apply/pallas_call | solution.py:312
  (1 shorter events, 0.0 us)
Async XLA Ops:
  0.0 27.3 %copy-start = (bf16[1,16,64,512]{3,2,1,0:T(8,128)(2,1)S(1)}, bf16[1,16,64,512]{3,2,1,0:T(8,128)(2,1)}, u32[]{:S(2)}) copy-start(bf16[1,16,64,512]{3,2,1,0:T(8,128)(2,1)} %param.7) | copy-start | bytes 3145732
  0.7 1.0 %copy-start.1 = (f32[64,2048]{1,0:T(8,128)S(1)}, f32[64,2048]{1,0:T(8,128)}, u32[]{:S(2)}) copy-start(f32[64,2048]{1,0:T(8,128)} %anom_hbm.1) | copy-start | bytes 1572868
  1.8 0.7 %copy-start.2 = (f32[2048]{0:T(1024)S(1)}, f32[2048]{0:T(1024)}, u32[]{:S(2)}) copy-start(f32[2048]{0:T(1024)} %param.9) | copy-start | bytes 24580
  2.5 0.7 %copy-start.3 = (f32[2048]{0:T(1024)S(1)}, f32[2048]{0:T(1024)}, u32[]{:S(2)}) copy-start(f32[2048]{0:T(1024)} %param.10) | copy-start | bytes 24580
  3.2 0.7 %copy-start.4 = (s32[2048]{0:T(1024)S(1)}, s32[2048]{0:T(1024)}, u32[]{:S(2)}) copy-start(s32[2048]{0:T(1024)} %param.11) | copy-start | bytes 24580
  3.9 0.7 %copy-start.5 = (f32[32]{0:T(128)S(1)}, f32[32]{0:T(128)}, u32[]{:S(2)}) copy-start(f32[32]{0:T(128)} %taper_ref.3) | copy-start | bytes 388
  7.9 19.9 %collective-permute-start.1 = (bf16[304,128]{1,0:T(8,128)(2,1)S(1)}, bf16[304,128]{1,0:T(8,128)(2,1)S(1)}, u32[]{:S(2)}, u32[]{:S(2)}) collective-permute-start(bf16[304,128]{1,0:T(8,128)(2,1)S(1)} %left_sums.1), channel_id=1, source_target_pairs={{4,0},{8,4},{12,8},{16,12},{20,16},{24,20},{28,24},{32,28},{36,32}... | collective-permute-start | bytes 233480 | tf_op jit(solution)/shard_map/ppermute | solution.py:284
  24.5 12.3 %collective-permute-start = (bf16[304,128]{1,0:T(8,128)(2,1)S(1)}, bf16[304,128]{1,0:T(8,128)(2,1)S(1)}, u32[]{:S(2)}, u32[]{:S(2)}) collective-permute-start(bf16[304,128]{1,0:T(8,128)(2,1)S(1)} %get-tuple-element.10), channel_id=1, source_target_pairs={{0,4},{4,8},{8,12},{12,16},{16,20},{20,24},{24,28},{28,32},{32,36}... | collective-permute-start | bytes 233480 | tf_op jit(solution)/shard_map/ppermute | solution.py:274

commit v2 on v1

--- a/solution.py
+++ b/solution.py
@@ -7,6 +7,7 @@
 
 NS_ITERS = 4
 K = 64
+REACH = 32
 U = 8
 W = 2 * K
 Q = 4
@@ -44,11 +45,15 @@
     lane = iota((1, W), 1)
     row, col = iota((K, W), 0), iota((K, W), 1) % K
 
+    def at(distance):
+        d = min(abs(distance), REACH - 1)
+        return taper_ref[d : d + 1, :]
+
     def same(f):
-        return taper_ref[min(abs(2 * f), 31)]
+        return at(2 * f)
 
     def crossed(f):
-        return jnp.where(lane < K, taper_ref[min(abs(2 * f + 1), 31)], taper_ref[min(abs(2 * f - 1), 31)])
+        return jnp.where(lane < K, at(2 * f + 1), at(2 * f - 1))
 
     out = [None] * U
     cross = {f: crossed(f) for f in range(1 - U + U * side, U + U * side)}
@@ -66,8 +71,8 @@
         line = jnp.sum(jnp.where(row == col, out[v + U // 2], 0.0), axis=0, keepdims=True)
         diag = jnp.where(sub == v, line, diag)
     vectors = []
-    for at in (GRAM, GRAM + U):
-        here = sums_ref[at : at + U, :]
+    for start in (GRAM, GRAM + U):
+        here = sums_ref[start : start + U, :]
         swapped = pltpu.roll(here, K, 1)
         total = jnp.zeros((U, W), F32)
         for d in range(U):
@@ -85,10 +90,10 @@
     out_ref[HALF:SENT, :] = rest
 
 
-def obs_kernel(count_hbm, taper_hbm, anom_hbm, innov_hbm, invv_hbm, col_hbm, sums_ref, right_ref,
-               count_ref, taper_ref, anom_ref, innov_ref, invv_ref, col_ref, sems):
+def obs_kernel(count_ref, taper_hbm, anom_hbm, innov_hbm, invv_hbm, col_hbm, sums_ref, table_ref, right_ref,
+               taper_ref, anom_ref, innov_ref, invv_ref, col_ref, sems):
     pairs = ((anom_hbm, anom_ref), (innov_hbm, innov_ref), (invv_hbm, invv_ref), (col_hbm, col_ref),
-             (count_hbm, count_ref), (taper_hbm, taper_ref))
+             (taper_hbm, taper_ref))
     copies = [pltpu.make_async_copy(a, b, sems.at[i]) for i, (a, b) in enumerate(pairs)]
     for copy in copies:
         copy.start()
@@ -127,26 +132,37 @@
             sums_ref[K * u : K * (u + 1), :] = sums[K * a : K * (a + 1), W * i : W * (i + 1)]
             sums_ref[GRAM + u : GRAM + u + 1, :] = vectors[a : a + 1, W * i : W * (i + 1)]
             sums_ref[GRAM + U + u : GRAM + U + u + 1, :] = vectors[Q + a : Q + a + 1, W * i : W * (i + 1)]
-    store(right_ref, mix(sums_ref, taper_ref, -1))
+    for d in range(REACH):
+        table_ref[d : d + 1, :] = jnp.full((1, W), taper_ref[d], F32)
+    store(right_ref, mix(sums_ref, table_ref, -1))
 
 
 def left_kernel(taper_ref, sums_ref, left_ref):
     store(left_ref, mix(sums_ref, taper_ref, 1))
 
 
+def put(out_ref, parts):
+    folded, bvec, mvec, diag = parts
+    out_ref[0:HALF, :] = folded
+    out_ref[HALF : HALF + 8, :] = bvec
+    out_ref[HALF + 8 : HALF + 16, :] = mvec
+    out_ref[HALF + 16 : HALF + 24, :] = diag
+
+
+def get(ref):
+    return [ref[0:HALF, :]] + [ref[HALF + 8 * i : HALF + 8 * (i + 1), :] for i in range(3)]
+
+
 def own_kernel(taper_ref, sums_ref, own_ref):
-    folded, bvec, mvec, diag = mix(sums_ref, taper_ref, 0)
-    own_ref[0:HALF, :] = folded
-    own_ref[HALF : HALF + 8, :] = bvec
-    own_ref[HALF + 8 : HALF + 16, :] = mvec
-    own_ref[HALF + 16 : HALF + 24, :] = diag
-
-
-def add_kernel(own_ref, before_ref, after_ref, out_ref):
-    parts = [own_ref[0:HALF, :]] + [own_ref[HALF + 8 * i : HALF + 8 * (i + 1), :] for i in range(3)]
-    for ref in (before_ref, after_ref):
-        parts = [x + y for x, y in zip(parts, decode(ref))]
-    store(out_ref, parts)
+    put(own_ref, mix(sums_ref, taper_ref, 0))
+
+
+def before_kernel(own_ref, before_ref, out_ref):
+    put(out_ref, [x + y for x, y in zip(get(own_ref), decode(before_ref))])
+
+
+def after_kernel(own_ref, after_ref, out_ref):
+    store(out_ref, [x + y for x, y in zip(get(own_ref), decode(after_ref))])
 
 
 def members_kernel(ens_ref, mean_ref, anom_ref):
@@ -249,48 +265,49 @@
     hbm = pl.BlockSpec(memory_space=pltpu.HBM)
     params = pltpu.CompilerParams(vmem_limit_bytes=48 * 2**20)
     sent = jax.ShapeDtypeStruct((SENT, W), BF16)
+    kept = jax.ShapeDtypeStruct((HALF + 24, W), F32)
 
     def cost(flops):
         return pl.CostEstimate(flops=flops, bytes_accessed=2**19, transcendentals=0)
 
-    sums, right = pl.pallas_call(
+    observed = (taper, obs_anomaly, innovation[None], inv_variance[None], obs_column[None])
+    sums, table, right = pl.pallas_call(
         obs_kernel,
-        out_shape=[jax.ShapeDtypeStruct((GRAM + 2 * U, W), F32), sent],
-        in_specs=[hbm] * 6,
-        out_specs=[vmem, vmem],
+        out_shape=[jax.ShapeDtypeStruct((GRAM + 2 * U, W), F32), jax.ShapeDtypeStruct((REACH, W), F32), sent],
+        in_specs=[smem] + [hbm] * 5,
+        out_specs=[vmem] * 3,
         scratch_shapes=[
-            pltpu.SMEM((1,), jnp.int32),
             pltpu.SMEM(taper.shape, F32),
             VMEM(obs_anomaly.shape, F32),
             VMEM((1, slots), F32),
             VMEM((1, slots), F32),
             VMEM((1, slots), jnp.int32),
-            pltpu.SemaphoreType.DMA((6,)),
+            pltpu.SemaphoreType.DMA((5,)),
         ],
         compiler_params=params,
         name="obs_sums",
-    )(obs_count, taper, obs_anomaly, innovation[None], inv_variance[None], obs_column[None])
+    )(obs_count, *(pltpu.with_memory_space_constraint(x, pltpu.HBM) for x in observed))
     count = lax.axis_size("space")
     before = lax.ppermute(right, "space", [(i, (i + 1) % count) for i in range(count)])
     left = pl.pallas_call(
         left_kernel,
         out_shape=sent,
-        in_specs=[smem, vmem],
+        in_specs=[vmem, vmem],
         out_specs=vmem,
         compiler_params=params,
         cost_estimate=cost(10**8),
         name="left_sums",
-    )(taper, sums)
+    )(table, sums)
     after = lax.ppermute(left, "space", [((i + 1) % count, i) for i in range(count)])
     own = pl.pallas_call(
         own_kernel,
-        out_shape=jax.ShapeDtypeStruct((HALF + 24, W), F32),
-        in_specs=[smem, vmem],
+        out_shape=kept,
+        in_specs=[vmem, vmem],
         out_specs=vmem,
         compiler_params=params,
         cost_estimate=cost(10**8),
         name="own_sums",
-    )(taper, sums)
+    )(table, sums)
     mean, anomalies = pl.pallas_call(
         members_kernel,
         out_shape=[jax.ShapeDtypeStruct((ncol, points), F32), jax.ShapeDtypeStruct((ncol * K, points), BF16)],
@@ -300,14 +317,22 @@
         cost_estimate=cost(10**8),
         name="member_means",
     )(ensemble[0])
+    own = pl.pallas_call(
+        before_kernel,
+        out_shape=kept,
+        in_specs=[vmem] * 2,
+        out_specs=vmem,
+        compiler_params=params,
+        name="add_before",
+    )(own, before)
     mixed = pl.pallas_call(
-        add_kernel,
+        after_kernel,
         out_shape=sent,
-        in_specs=[vmem] * 3,
+        in_specs=[vmem] * 2,
         out_specs=vmem,
         compiler_params=params,
-        name="add_sides",
-    )(own, before, after)
+        name="add_after",
+    )(own, after)
     parts = lax.all_gather(mixed, "lag")
     out = pl.pallas_call(
         finish_kernel,

time: 48.8 us -> 35 us (0.72)
  waiting for transfers between devices: 9.03 us -> 0.61 us
  local copies, waits for them, and re-layouts: 3.78 us -> 0.01 us
  blocking collectives: 8.16 us -> 7.36 us
  Pallas kernels: 8.13 us -> 7.48 us
    ppermute x1, waiting for transfers between devices: 9.03 us -> 0.01 us  [on_device(): lax.ppermute(right, 'space', [(i, (i + 1) % count) for i in range(count)])]
    unnamed x12 -> x2, local copies, waits for them, and re-layouts: 3.78 us -> 0.01 us
    ppermute x1, starting transfers between devices: 16.6 us -> 14.5 us  [on_device(): lax.ppermute(left, 'space', [((i + 1) % count, i) for i in range(count)])]
    ppermute x1, starting transfers between devices: 1.92 us -> 4.03 us  [on_device(): lax.ppermute(right, 'space', [(i, (i + 1) % count) for i in range(count)])]
    pallas_call x3 -> x4, Pallas kernels: 1.87 us -> 0.79 us  [the longest x1 0.38 us: on_device(): pl.pallas_call(left_kernel, out_shape=sent, in_specs=[vmem, vmem], out_sp...]
    all_gather x1, blocking collectives: 8.16 us -> 7.36 us  [on_device(): parts = lax.all_gather(mixed, 'lag')]
    ppermute x1, waiting for transfers between devices: 0.01 us -> 0.61 us  [on_device(): lax.ppermute(left, 'space', [((i + 1) % count, i) for i in range(count)])]
where the time goes in v2:
time: 35 us; the launch traced here: 34.8 us
  starting transfers between devices  18.5 us (53%)
  Pallas kernels  7.48 us (21%)
  blocking collectives  7.36 us (21%)
  between operations  0.81 us (2%)
  waiting for transfers between devices  0.61 us (2%)
    ppermute x1, starting transfers between devices, on_device(): lax.ppermute(left, 'space', [((i + 1) % count, i) for i in range(count)])  14.5 us
    all_gather x1, blocking collectives, on_device(): parts = lax.all_gather(mixed, 'lag')  7.36 us
    ppermute x1, starting transfers between devices, on_device(): lax.ppermute(right, 'space', [(i, (i + 1) % count) for i in range(count)])  4.03 us
    pallas_call x1, Pallas kernels, on_device(): pl.pallas_call(finish_kernel, out_shape=jax.ShapeDtypeStruct((ncol, K, po...  3.48 us
    pallas_call x1, Pallas kernels, on_device(): pl.pallas_call(obs_kernel, out_shape=[jax.ShapeDtypeStruct((GRAM + 2 * U,...  2.82 us
  transfers between devices with their start and end apart: 2, of which 1 were waited for; matrix products, arithmetic and copies ran while one was open for 0% of the time, Pallas kernels for 3%

profile of v2, /device:TPU:1, one launch (start us, length us, event | category | flops | bytes accessed | tf_op | source)
XLA Modules:
  0.0 34.8 jit_solution(6865865893912014369)
XLA Ops:
  0.0 0.0 copy-start
  0.7 2.8 %obs_sums.1 = (f32[528,128]{1,0:T(8,128)S(1)}, f32[32,128]{1,0:T(8,128)S(1)}, bf16[304,128]{1,0:T(8,128)(2,1)S(1)}) custom-call(s32[1]{0:T(128)S(6)} %copy.8.count_ref, f32[32]{0:T(128)} %taper_hbm.1, f32[64,2048]{1,0:T(8,128)} %anom_hbm.1, f32[1,2048]{1,0:T(1,128)} %bitcast.8, f32[1,2048]{1,0:T(1,128)} %bitcast.9, s32[1,2048]{1,0:T(1,128)} %bitcast.10), custom_call_target="tpu_custom_call" | custom-call | tf_op jit(solution)/shard_map/obs_sums/pallas_call | solution.py:274
  3.6 4.0 %collective-permute-start = (bf16[304,128]{1,0:T(8,128)(2,1)S(1)}, bf16[304,128]{1,0:T(8,128)(2,1)S(1)}, u32[]{:S(2)}, u32[]{:S(2)}) collective-permute-start(bf16[304,128]{1,0:T(8,128)(2,1)S(1)} %get-tuple-element.12), channel_id=1, source_target_pairs={{0,4},{4,8},{8,12},{12,16},{16,20},{20,24},{24,28},{28,32},{32,36}... | collective-permute-start | bytes 233480 | tf_op jit(solution)/shard_map/ppermute | solution.py:291
  7.6 0.4 %left_sums.1 = bf16[304,128]{1,0:T(8,128)(2,1)S(1)} custom-call(f32[32,128]{1,0:T(8,128)S(1)} %get-tuple-element.10.taper_ref, f32[528,128]{1,0:T(8,128)S(1)} %get-tuple-element.11.sums_ref), custom_call_target="tpu_custom_call" | custom-call | flops 100000000 | bytes 524288 | tf_op jit(solution)/shard_map/left_sums/pallas_call | solution.py:292
  8.0 14.5 %collective-permute-start.1 = (bf16[304,128]{1,0:T(8,128)(2,1)S(1)}, bf16[304,128]{1,0:T(8,128)(2,1)S(1)}, u32[]{:S(2)}, u32[]{:S(2)}) collective-permute-start(bf16[304,128]{1,0:T(8,128)(2,1)S(1)} %left_sums.1), channel_id=1, source_target_pairs={{4,0},{8,4},{12,8},{16,12},{20,16},{24,20},{28,24},{32,28},{36,32}... | collective-permute-start | bytes 233480 | tf_op jit(solution)/shard_map/ppermute | solution.py:301
  22.5 0.4 %own_sums.1.own_ref = f32[280,128]{1,0:T(8,128)S(1)} custom-call(f32[32,128]{1,0:T(8,128)S(1)} %get-tuple-element.10.taper_ref, f32[528,128]{1,0:T(8,128)S(1)} %get-tuple-element.11.sums_ref), custom_call_target="tpu_custom_call" | custom-call | flops 100000000 | bytes 524288 | tf_op jit(solution)/shard_map/own_sums/pallas_call | solution.py:302
  22.8 0.0 copy-done
  22.9 0.4 %member_means.1 = (f32[16,512]{1,0:T(8,128)S(1)}, bf16[1024,512]{1,0:T(8,128)(2,1)S(1)}) custom-call(bf16[16,64,512]{2,1,0:T(8,128)(2,1)S(1)} %bitcast.7), custom_call_target="tpu_custom_call" | custom-call | flops 100000000 | bytes 524288 | tf_op jit(solution)/shard_map/member_means/pallas_call | solution.py:311
  23.3 0.0 collective-permute-done.before_ref
  23.3 0.6 %collective-permute-done.1.after_ref = bf16[304,128]{1,0:T(8,128)(2,1)S(1)} collective-permute-done((bf16[304,128]{1,0:T(8,128)(2,1)S(1)}, bf16[304,128]{1,0:T(8,128)(2,1)S(1)}, u32[]{:S(2)}, u32[]{:S(2)}) %collective-permute-start.1) | collective-permute-done | bytes 77856 | tf_op jit(solution)/shard_map/ppermute | solution.py:301
  23.9 7.4 %all-gather = bf16[1216,128]{1,0:T(8,128)(2,1)S(1)} all-gather(bf16[304,128]{1,0:T(8,128)(2,1)S(1)} %add_after.1), channel_id=2, replica_groups=mesh['space'=128,'lag'=4] {'lag'}, dimensions={0}, use_global_device_ids=true | all-gather | bytes 389120 | tf_op jit(solution)/shard_map/all_gather | solution.py:336
  31.3 3.5 %transform_apply.1 = bf16[16,64,512]{2,1,0:T(8,128)(2,1)} custom-call(bf16[4,304,128]{2,1,0:T(8,128)(2,1)S(1)} %bitcast.6, f32[16,512]{1,0:T(8,128)S(1)} %get-tuple-element.13.mean_ref, bf16[1024,512]{1,0:T(8,128)(2,1)S(1)} %get-tuple-element.14.anom_ref), custom_call_target="tpu_custom_call" | custom-call | tf_op jit(solution)/shard_map/transform_apply/pallas_call | solution.py:337
  (2 shorter events, 0.0 us)
Async XLA Ops:
  0.0 22.8 %copy-start = (bf16[1,16,64,512]{3,2,1,0:T(8,128)(2,1)S(1)}, bf16[1,16,64,512]{3,2,1,0:T(8,128)(2,1)}, u32[]{:S(2)}) copy-start(bf16[1,16,64,512]{3,2,1,0:T(8,128)(2,1)} %param.7) | copy-start | bytes 3145732
  3.6 19.7 %collective-permute-start = (bf16[304,128]{1,0:T(8,128)(2,1)S(1)}, bf16[304,128]{1,0:T(8,128)(2,1)S(1)}, u32[]{:S(2)}, u32[]{:S(2)}) collective-permute-start(bf16[304,128]{1,0:T(8,128)(2,1)S(1)} %get-tuple-element.12), channel_id=1, source_target_pairs={{0,4},{4,8},{8,12},{12,16},{16,20},{20,24},{24,28},{28,32},{32,36}... | collective-permute-start | bytes 233480 | tf_op jit(solution)/shard_map/ppermute | solution.py:291
  8.0 15.9 %collective-permute-start.1 = (bf16[304,128]{1,0:T(8,128)(2,1)S(1)}, bf16[304,128]{1,0:T(8,128)(2,1)S(1)}, u32[]{:S(2)}, u32[]{:S(2)}) collective-permute-start(bf16[304,128]{1,0:T(8,128)(2,1)S(1)} %left_sums.1), channel_id=1, source_target_pairs={{4,0},{8,4},{12,8},{16,12},{20,16},{24,20},{28,24},{32,28},{36,32}... | collective-permute-start | bytes 233480 | tf_op jit(solution)/shard_map/ppermute | solution.py:301

commit v3 on v2

--- a/solution.py
+++ b/solution.py
@@ -97,16 +97,20 @@
     copies = [pltpu.make_async_copy(a, b, sems.at[i]) for i, (a, b) in enumerate(pairs)]
     for copy in copies:
         copy.start()
-    for copy in copies:
+    for copy in copies[1:]:
         copy.wait()
     slots = anom_ref.shape[1]
+    for d in range(REACH):
+        table_ref[d : d + 1, :] = jnp.full((1, W), taper_ref[d], F32)
     rinv = jnp.where(iota((1, slots), 1) < count_ref[0], invv_ref[...], 0.0)
     column = col_ref[...]
     outer, inner = column // Q, column % Q
+    scaled = [jnp.where(outer == a, rinv, 0.0) for a in range(Q)]
+    copies[0].wait()
     whole = anom_ref[...]
     mean = jnp.sum(whole, axis=0, keepdims=True) * (1.0 / K)
     anom = whole - mean
-    left = [anom * jnp.where(outer == a, rinv, 0.0) for a in range(Q)]
+    left = [anom * scaled[a] for a in range(Q)]
     row = iota((16, slots), 0)
     rows = jnp.where(row < Q, innov_ref[...] * rinv, jnp.where(row < 2 * Q, mean * rinv, 0.0))
     left.append(jnp.where(row % Q == outer, rows, 0.0))
@@ -117,7 +121,9 @@
     def dot(a, b):
         return lax.dot_general(a, b, (((1,), (1,)), ((), ())), preferred_element_type=F32)
 
-    sums = dot(lhi, rhi) + (dot(lhi, rlo) + dot(llo, rhi))
+    n = Q * K + 16
+    both = dot(jnp.concatenate([lhi, llo], axis=0), rhi)
+    sums = both[:n] + (both[n:] + dot(lhi, rlo))
     thi, tlo = lhi[Q * K :], llo[Q * K :]
     scalars = dot(thi, mhi) + (dot(thi, mlo) + dot(tlo, mhi))
     lane = iota((1, Q * K), 1) // K
@@ -132,8 +138,6 @@
             sums_ref[K * u : K * (u + 1), :] = sums[K * a : K * (a + 1), W * i : W * (i + 1)]
             sums_ref[GRAM + u : GRAM + u + 1, :] = vectors[a : a + 1, W * i : W * (i + 1)]
             sums_ref[GRAM + U + u : GRAM + U + u + 1, :] = vectors[Q + a : Q + a + 1, W * i : W * (i + 1)]
-    for d in range(REACH):
-        table_ref[d : d + 1, :] = jnp.full((1, W), taper_ref[d], F32)
     store(right_ref, mix(sums_ref, table_ref, -1))
 
 
@@ -174,34 +178,36 @@
 
 
 def finish_kernel(parts_ref, mean_ref, anom_ref, out_ref, buf, sems):
-    width = Q * K
-    groups = U * W // width
+    width = W
+    groups = U
+    n = W // K
     lane = iota((1, width), 1) // K
     diagonal = iota((width, width), 0) // K == iota((width, width), 1) // K
     eye = jnp.where(iota((K, width), 0) == iota((K, width), 1) % K, 1.0, 0.0)
     row, col = iota((K, W), 0), iota((K, W), 1) % K
+    left_half = iota((K, W), 1) < K
 
     def spread(x):
-        tall = jnp.concatenate([x] * Q, axis=0)
+        tall = jnp.concatenate([x] * n, axis=0)
         return jnp.where(diagonal, tall, jnp.zeros_like(tall))
 
     def dot(a, b):
         return jnp.dot(a, b, preferred_element_type=F32)
 
     def times(left, right):
-        n = len(left)
+        count = len(left)
         parts = [halves(x) for x in left]
         hi = [p[0] for p in parts]
         lo = [p[1] for p in parts]
         rhi, rlo = halves(right)
         first = dot(jnp.concatenate(hi + lo, axis=0), spread(rhi))
         second = dot(jnp.concatenate(hi, axis=0), spread(rlo))
-        out = first[: n * K] + (first[n * K :] + second)
-        return [out[i * K : (i + 1) * K] for i in range(n)]
+        out = first[: count * K] + (first[count * K :] + second)
+        return [out[i * K : (i + 1) * K] for i in range(count)]
 
     def lane_sums(x):
         out = jnp.zeros_like(x)
-        for cc in range(Q):
+        for cc in range(n):
             out = jnp.where(lane == cc, jnp.sum(jnp.where(lane == cc, x, 0.0), axis=1, keepdims=True), out)
         return out
 
@@ -212,22 +218,31 @@
     units = [None] * U
     for v in range(U // 2):
         here = folded[K * v : K * (v + 1)]
-        tall = jnp.transpose(here)
-        turned = jnp.concatenate([tall[:K], tall[K:]], axis=1)
+        if v % 2 == 0:
+            square = jnp.transpose(folded[K * v : K * (v + 2)])
+            upper, lower = square[:K], square[K:]
+            turned = jnp.where(left_half, upper, pltpu.roll(lower, K, 1))
+        else:
+            turned = jnp.where(left_half, pltpu.roll(upper, K, 1), lower)
         units[v] = jnp.where(row <= col, here, turned)
         units[v + U // 2] = jnp.where(row == col, diag[v : v + 1], jnp.where(row > col, here, turned))
-    pairs = [slice(2 * g, 2 * g + 2) for g in range(groups)]
-
-    def wide(vec, g):
-        return jnp.concatenate([vec[2 * g : 2 * g + 1], vec[2 * g + 1 : 2 * g + 2]], axis=1)
-
-    bvec = [wide(bvec, g) for g in range(groups)]
-    mvec = [wide(mvec, g) for g in range(groups)]
+    bvec = [bvec[g : g + 1] for g in range(groups)]
+    mvec = [mvec[g : g + 1] for g in range(groups)]
+    parts = []
+    for g in range(groups):
+        line = eye * mvec[g]
+        high, low = halves(line)
+        parts += [high, low, (line - high.astype(F32) - low.astype(F32)).astype(BF16)]
+    ones = jnp.where(diagonal, 1.0, 0.0).astype(BF16)
+    across = dot(jnp.concatenate(parts, axis=0), ones)
+    across = [sum(across[K * (3 * g + i) : K * (3 * g + i + 1)] for i in range(3)) for g in range(groups)]
     amat = [
-        jnp.concatenate(units[pairs[g]], axis=1) + mvec[g] + lane_sums(eye * mvec[g]) + (K - 1.0) * eye
+        units[g] + mvec[g] + across[g] + (K - 1.0) * eye
         for g in range(groups)
     ]
-    scale = [jnp.sqrt(lane_sums(jnp.sum(a * a, axis=0, keepdims=True))) for a in amat]
+    norms = jnp.concatenate([jnp.sum(a * a, axis=0, keepdims=True) for a in amat], axis=0)
+    scale = jnp.sqrt(lane_sums(norms))
+    scale = [scale[g : g + 1] for g in range(groups)]
     yval = [a / s for a, s in zip(amat, scale)]
     mval = [1.5 * eye - 0.5 * y for y in yval]
     zval = mval
@@ -248,10 +263,10 @@
     copies = []
     for g in range(groups):
         mixed = dot(spread(weights[g]), anom_ref[width * g : width * (g + 1), :])
-        for cc in range(Q):
-            c = Q * g + cc
+        for cc in range(n):
+            c = n * g + cc
             buf[c] = (mean_ref[c : c + 1, :] + mixed[K * cc : K * (cc + 1)]).astype(BF16)
-        copies.append(pltpu.make_async_copy(buf.at[pl.ds(Q * g, Q)], out_ref.at[pl.ds(Q * g, Q)], sems.at[g]))
+        copies.append(pltpu.make_async_copy(buf.at[pl.ds(n * g, n)], out_ref.at[pl.ds(n * g, n)], sems.at[g]))
         copies[-1].start()
     for copy in copies:
         copy.wait()
@@ -339,7 +354,7 @@
         out_shape=jax.ShapeDtypeStruct((ncol, K, points), BF16),
         in_specs=[vmem] * 3,
         out_specs=pl.BlockSpec(memory_space=pl.ANY),
-        scratch_shapes=[VMEM((ncol, K, points), BF16), pltpu.SemaphoreType.DMA((ncol // Q,))],
+        scratch_shapes=[VMEM((ncol, K, points), BF16), pltpu.SemaphoreType.DMA((U,))],
         compiler_params=params,
         name="transform_apply",
     )(parts, mean, anomalies)

time: 35 us -> 34.4 us (0.983)
  Pallas kernels: 7.48 us -> 6.95 us
where the time goes in v3:
time: 34.4 us; the launch traced here: 34.2 us
  starting transfers between devices  18.5 us (54%)
  blocking collectives  7.36 us (21%)
  Pallas kernels  6.95 us (20%)
  between operations  0.81 us (2%)
  waiting for transfers between devices  0.61 us (2%)
    ppermute x1, starting transfers between devices, on_device(): lax.ppermute(left, 'space', [((i + 1) % count, i) for i in range(count)])  14.5 us
    all_gather x1, blocking collectives, on_device(): parts = lax.all_gather(mixed, 'lag')  7.36 us
    ppermute x1, starting transfers between devices, on_device(): lax.ppermute(right, 'space', [(i, (i + 1) % count) for i in range(count)])  4.03 us
    pallas_call x1, Pallas kernels, on_device(): pl.pallas_call(finish_kernel, out_shape=jax.ShapeDtypeStruct((ncol, K, po...  3.14 us
    pallas_call x1, Pallas kernels, on_device(): pl.pallas_call(obs_kernel, out_shape=[jax.ShapeDtypeStruct((GRAM + 2 * U,...  2.62 us
  transfers between devices with their start and end apart: 2, of which 1 were waited for; matrix products, arithmetic and copies ran while one was open for 0% of the time, Pallas kernels for 3%

profile of v3, /device:TPU:1, one launch (start us, length us, event | category | flops | bytes accessed | tf_op | source)
XLA Modules:
  0.0 34.2 jit_solution(9762207936033956693)
XLA Ops:
  0.0 0.0 copy-start
  0.7 2.6 %obs_sums.1 = (f32[528,128]{1,0:T(8,128)S(1)}, f32[32,128]{1,0:T(8,128)S(1)}, bf16[304,128]{1,0:T(8,128)(2,1)S(1)}) custom-call(s32[1]{0:T(128)S(6)} %copy.8.count_ref, f32[32]{0:T(128)} %taper_hbm.1, f32[64,2048]{1,0:T(8,128)} %anom_hbm.1, f32[1,2048]{1,0:T(1,128)} %bitcast.8, f32[1,2048]{1,0:T(1,128)} %bitcast.9, s32[1,2048]{1,0:T(1,128)} %bitcast.10), custom_call_target="tpu_custom_call" | custom-call | tf_op jit(solution)/shard_map/obs_sums/pallas_call | solution.py:289
  3.4 4.0 %collective-permute-start = (bf16[304,128]{1,0:T(8,128)(2,1)S(1)}, bf16[304,128]{1,0:T(8,128)(2,1)S(1)}, u32[]{:S(2)}, u32[]{:S(2)}) collective-permute-start(bf16[304,128]{1,0:T(8,128)(2,1)S(1)} %get-tuple-element.12), channel_id=1, source_target_pairs={{0,4},{4,8},{8,12},{12,16},{16,20},{20,24},{24,28},{28,32},{32,36}... | collective-permute-start | bytes 233480 | tf_op jit(solution)/shard_map/ppermute | solution.py:306
  7.4 0.4 %left_sums.1 = bf16[304,128]{1,0:T(8,128)(2,1)S(1)} custom-call(f32[32,128]{1,0:T(8,128)S(1)} %get-tuple-element.10.taper_ref, f32[528,128]{1,0:T(8,128)S(1)} %get-tuple-element.11.sums_ref), custom_call_target="tpu_custom_call" | custom-call | flops 100000000 | bytes 524288 | tf_op jit(solution)/shard_map/left_sums/pallas_call | solution.py:307
  7.8 14.5 %collective-permute-start.1 = (bf16[304,128]{1,0:T(8,128)(2,1)S(1)}, bf16[304,128]{1,0:T(8,128)(2,1)S(1)}, u32[]{:S(2)}, u32[]{:S(2)}) collective-permute-start(bf16[304,128]{1,0:T(8,128)(2,1)S(1)} %left_sums.1), channel_id=1, source_target_pairs={{4,0},{8,4},{12,8},{16,12},{20,16},{24,20},{28,24},{32,28},{36,32}... | collective-permute-start | bytes 233480 | tf_op jit(solution)/shard_map/ppermute | solution.py:316
  22.3 0.4 %own_sums.1.own_ref = f32[280,128]{1,0:T(8,128)S(1)} custom-call(f32[32,128]{1,0:T(8,128)S(1)} %get-tuple-element.10.taper_ref, f32[528,128]{1,0:T(8,128)S(1)} %get-tuple-element.11.sums_ref), custom_call_target="tpu_custom_call" | custom-call | flops 100000000 | bytes 524288 | tf_op jit(solution)/shard_map/own_sums/pallas_call | solution.py:317
  22.6 0.0 copy-done
  22.7 0.4 %member_means.1 = (f32[16,512]{1,0:T(8,128)S(1)}, bf16[1024,512]{1,0:T(8,128)(2,1)S(1)}) custom-call(bf16[16,64,512]{2,1,0:T(8,128)(2,1)S(1)} %bitcast.7), custom_call_target="tpu_custom_call" | custom-call | flops 100000000 | bytes 524288 | tf_op jit(solution)/shard_map/member_means/pallas_call | solution.py:326
  23.1 0.0 collective-permute-done.before_ref
  23.1 0.6 %collective-permute-done.1.after_ref = bf16[304,128]{1,0:T(8,128)(2,1)S(1)} collective-permute-done((bf16[304,128]{1,0:T(8,128)(2,1)S(1)}, bf16[304,128]{1,0:T(8,128)(2,1)S(1)}, u32[]{:S(2)}, u32[]{:S(2)}) %collective-permute-start.1) | collective-permute-done | bytes 77856 | tf_op jit(solution)/shard_map/ppermute | solution.py:316
  23.7 7.4 %all-gather = bf16[1216,128]{1,0:T(8,128)(2,1)S(1)} all-gather(bf16[304,128]{1,0:T(8,128)(2,1)S(1)} %add_after.1), channel_id=2, replica_groups=mesh['space'=128,'lag'=4] {'lag'}, dimensions={0}, use_global_device_ids=true | all-gather | bytes 389120 | tf_op jit(solution)/shard_map/all_gather | solution.py:351
  31.1 3.1 %transform_apply.1 = bf16[16,64,512]{2,1,0:T(8,128)(2,1)} custom-call(bf16[4,304,128]{2,1,0:T(8,128)(2,1)S(1)} %bitcast.6, f32[16,512]{1,0:T(8,128)S(1)} %get-tuple-element.13.mean_ref, bf16[1024,512]{1,0:T(8,128)(2,1)S(1)} %get-tuple-element.14.anom_ref), custom_call_target="tpu_custom_call" | custom-call | tf_op jit(solution)/shard_map/transform_apply/pallas_call | solution.py:352
  (2 shorter events, 0.0 us)
Async XLA Ops:
  0.0 22.6 %copy-start = (bf16[1,16,64,512]{3,2,1,0:T(8,128)(2,1)S(1)}, bf16[1,16,64,512]{3,2,1,0:T(8,128)(2,1)}, u32[]{:S(2)}) copy-start(bf16[1,16,64,512]{3,2,1,0:T(8,128)(2,1)} %param.7) | copy-start | bytes 3145732
  3.4 19.7 %collective-permute-start = (bf16[304,128]{1,0:T(8,128)(2,1)S(1)}, bf16[304,128]{1,0:T(8,128)(2,1)S(1)}, u32[]{:S(2)}, u32[]{:S(2)}) collective-permute-start(bf16[304,128]{1,0:T(8,128)(2,1)S(1)} %get-tuple-element.12), channel_id=1, source_target_pairs={{0,4},{4,8},{8,12},{12,16},{16,20},{20,24},{24,28},{28,32},{32,36}... | collective-permute-start | bytes 233480 | tf_op jit(solution)/shard_map/ppermute | solution.py:306
  7.8 15.9 %collective-permute-start.1 = (bf16[304,128]{1,0:T(8,128)(2,1)S(1)}, bf16[304,128]{1,0:T(8,128)(2,1)S(1)}, u32[]{:S(2)}, u32[]{:S(2)}) collective-permute-start(bf16[304,128]{1,0:T(8,128)(2,1)S(1)} %left_sums.1), channel_id=1, source_target_pairs={{4,0},{8,4},{12,8},{16,12},{20,16},{24,20},{28,24},{32,28},{36,32}... | collective-permute-start | bytes 233480 | tf_op jit(solution)/shard_map/ppermute | solution.py:316

commit v4 on v3

--- a/solution.py
+++ b/solution.py
@@ -90,23 +90,18 @@
     out_ref[HALF:SENT, :] = rest
 
 
-def obs_kernel(count_ref, taper_hbm, anom_hbm, innov_hbm, invv_hbm, col_hbm, sums_ref, table_ref, right_ref,
-               taper_ref, anom_ref, innov_ref, invv_ref, col_ref, sems):
-    pairs = ((anom_hbm, anom_ref), (innov_hbm, innov_ref), (invv_hbm, invv_ref), (col_hbm, col_ref),
-             (taper_hbm, taper_ref))
-    copies = [pltpu.make_async_copy(a, b, sems.at[i]) for i, (a, b) in enumerate(pairs)]
-    for copy in copies:
-        copy.start()
-    for copy in copies[1:]:
-        copy.wait()
+def lanes_kernel(out_ref):
+    out_ref[...] = iota(out_ref.shape, 1)
+
+
+def obs_kernel(count_ref, taper_ref, lanes_ref, anom_ref, innov_ref, invv_ref, col_ref, sums_ref, table_ref, right_ref):
     slots = anom_ref.shape[1]
     for d in range(REACH):
         table_ref[d : d + 1, :] = jnp.full((1, W), taper_ref[d], F32)
-    rinv = jnp.where(iota((1, slots), 1) < count_ref[0], invv_ref[...], 0.0)
+    rinv = jnp.where(lanes_ref[0:1, :] < count_ref[0], invv_ref[...], 0.0)
     column = col_ref[...]
     outer, inner = column // Q, column % Q
     scaled = [jnp.where(outer == a, rinv, 0.0) for a in range(Q)]
-    copies[0].wait()
     whole = anom_ref[...]
     mean = jnp.sum(whole, axis=0, keepdims=True) * (1.0 / K)
     anom = whole - mean
@@ -243,10 +238,10 @@
     norms = jnp.concatenate([jnp.sum(a * a, axis=0, keepdims=True) for a in amat], axis=0)
     scale = jnp.sqrt(lane_sums(norms))
     scale = [scale[g : g + 1] for g in range(groups)]
-    yval = [a / s for a, s in zip(amat, scale)]
-    mval = [1.5 * eye - 0.5 * y for y in yval]
-    zval = mval
-    yval = [times([y], m)[0] for y, m in zip(yval, mval)]
+    square = [times([a], a)[0] for a in amat]
+    inverse = [1.0 / s for s in scale]
+    zval = [1.5 * eye - (0.5 * i) * a for a, i in zip(amat, inverse)]
+    yval = [(1.5 * i) * a - (0.5 * i * i) * q for a, i, q in zip(amat, inverse, square)]
     for step in range(1, NS_ITERS):
         prod = [times([z], y)[0] for z, y in zip(zval, yval)]
         mval = [1.5 * eye - 0.5 * p for p in prod]
@@ -258,8 +253,8 @@
     weights = []
     for g in range(groups):
         inner = lane_sums(zval[g] * bvec[g])
-        shift = jnp.sum(zval[g] * inner, axis=0, keepdims=True) / scale[g]
-        weights.append((zval[g] * (jnp.sqrt(K - 1.0) / jnp.sqrt(scale[g])) + shift).astype(BF16))
+        shift = jnp.sum(zval[g] * inner, axis=0, keepdims=True) * inverse[g]
+        weights.append((zval[g] * jnp.sqrt((K - 1.0) * inverse[g]) + shift).astype(BF16))
     copies = []
     for g in range(groups):
         mixed = dot(spread(weights[g]), anom_ref[width * g : width * (g + 1), :])
@@ -277,7 +272,6 @@
     _, ncol, _, points = ensemble.shape
     vmem = pl.BlockSpec(memory_space=VMEM)
     smem = pl.BlockSpec(memory_space=pltpu.SMEM)
-    hbm = pl.BlockSpec(memory_space=pltpu.HBM)
     params = pltpu.CompilerParams(vmem_limit_bytes=48 * 2**20)
     sent = jax.ShapeDtypeStruct((SENT, W), BF16)
     kept = jax.ShapeDtypeStruct((HALF + 24, W), F32)
@@ -285,23 +279,22 @@
     def cost(flops):
         return pl.CostEstimate(flops=flops, bytes_accessed=2**19, transcendentals=0)
 
-    observed = (taper, obs_anomaly, innovation[None], inv_variance[None], obs_column[None])
+    lanes = pl.pallas_call(
+        lanes_kernel,
+        out_shape=jax.ShapeDtypeStruct((8, slots), jnp.int32),
+        out_specs=vmem,
+        compiler_params=params,
+        cost_estimate=cost(10**9),
+        name="lane_numbers",
+    )()
     sums, table, right = pl.pallas_call(
         obs_kernel,
         out_shape=[jax.ShapeDtypeStruct((GRAM + 2 * U, W), F32), jax.ShapeDtypeStruct((REACH, W), F32), sent],
-        in_specs=[smem] + [hbm] * 5,
+        in_specs=[smem] * 2 + [vmem] * 5,
         out_specs=[vmem] * 3,
-        scratch_shapes=[
-            pltpu.SMEM(taper.shape, F32),
-            VMEM(obs_anomaly.shape, F32),
-            VMEM((1, slots), F32),
-            VMEM((1, slots), F32),
-            VMEM((1, slots), jnp.int32),
-            pltpu.SemaphoreType.DMA((5,)),
-        ],
         compiler_params=params,
         name="obs_sums",
-    )(obs_count, *(pltpu.with_memory_space_constraint(x, pltpu.HBM) for x in observed))
+    )(obs_count, taper, lanes, obs_anomaly, innovation[None], inv_variance[None], obs_column[None])
     count = lax.axis_size("space")
     before = lax.ppermute(right, "space", [(i, (i + 1) % count) for i in range(count)])
     left = pl.pallas_call(

time: 34.4 us -> 33.9 us (0.985)
  Pallas kernels: 6.95 us -> 6.13 us
    pallas_call x1, Pallas kernels: 2.62 us -> 2.1 us  [on_device(): pl.pallas_call(obs_kernel, out_shape=[jax.ShapeDtypeStruct((GRAM + 2 * U,...]
where the time goes in v4:
time: 33.9 us; the launch traced here: 33.7 us
  starting transfers between devices  18.5 us (55%)
  blocking collectives  7.36 us (22%)
  Pallas kernels  6.13 us (18%)
  between operations  0.86 us (3%)
  waiting for transfers between devices  0.61 us (2%)
    ppermute x1, starting transfers between devices, on_device(): lax.ppermute(left, 'space', [((i + 1) % count, i) for i in range(count)])  14.5 us
    all_gather x1, blocking collectives, on_device(): parts = lax.all_gather(mixed, 'lag')  7.36 us
    ppermute x1, starting transfers between devices, on_device(): lax.ppermute(right, 'space', [(i, (i + 1) % count) for i in range(count)])  4.03 us
    pallas_call x1, Pallas kernels, on_device(): pl.pallas_call(finish_kernel, out_shape=jax.ShapeDtypeStruct((ncol, K, po...  2.84 us
    pallas_call x1, Pallas kernels, on_device(): pl.pallas_call(obs_kernel, out_shape=[jax.ShapeDtypeStruct((GRAM + 2 * U,...  2.1 us
  transfers between devices with their start and end apart: 2, of which 1 were waited for; matrix products, arithmetic and copies ran while one was open for 0% of the time, Pallas kernels for 3%

profile of v4, /device:TPU:1, one launch (start us, length us, event | category | flops | bytes accessed | tf_op | source)
XLA Modules:
  0.0 33.7 jit_solution(16286604324250546195)
XLA Ops:
  0.0 0.0 copy-start.1
  0.0 0.0 copy-start.2
  0.0 0.0 copy-start.3
  0.0 0.0 copy-start.4
  0.0 0.0 copy-start.5
  0.0 0.0 copy-start
  0.8 0.2 copy-done.1
  1.0 0.0 copy-done.2
  1.0 0.0 copy-done.3
  1.0 0.0 copy-done.4
  1.1 0.0 copy-done.5
  1.1 2.1 %obs_sums.1 = (f32[528,128]{1,0:T(8,128)S(1)}, f32[32,128]{1,0:T(8,128)S(1)}, bf16[304,128]{1,0:T(8,128)(2,1)S(1)}) custom-call(s32[1]{0:T(128)S(6)} %copy.8.count_ref, f32[32]{0:T(128)S(1)} %copy-done.5, s32[8,2048]{1,0:T(8,128)S(1)} %lane_numbers.1.lanes_ref, f32[64,2048]{1,0:T(8,128)S(1)} %copy-done.1, f32[1,2048]{1,0:T(1,128)S(1)} %bitcast.8, ...), custom_call_target="tpu_custom_call" | custom-call | tf_op jit(solution)/shard_map/obs_sums/pallas_call | solution.py:290
  3.2 4.0 %collective-permute-start = (bf16[304,128]{1,0:T(8,128)(2,1)S(1)}, bf16[304,128]{1,0:T(8,128)(2,1)S(1)}, u32[]{:S(2)}, u32[]{:S(2)}) collective-permute-start(bf16[304,128]{1,0:T(8,128)(2,1)S(1)} %get-tuple-element.12), channel_id=1, source_target_pairs={{0,4},{4,8},{8,12},{12,16},{16,20},{20,24},{24,28},{28,32},{32,36}... | collective-permute-start | bytes 233480 | tf_op jit(solution)/shard_map/ppermute | solution.py:299
  7.2 0.4 %left_sums.1 = bf16[304,128]{1,0:T(8,128)(2,1)S(1)} custom-call(f32[32,128]{1,0:T(8,128)S(1)} %get-tuple-element.10.taper_ref, f32[528,128]{1,0:T(8,128)S(1)} %get-tuple-element.11.sums_ref), custom_call_target="tpu_custom_call" | custom-call | flops 100000000 | bytes 524288 | tf_op jit(solution)/shard_map/left_sums/pallas_call | solution.py:300
  7.6 14.5 %collective-permute-start.1 = (bf16[304,128]{1,0:T(8,128)(2,1)S(1)}, bf16[304,128]{1,0:T(8,128)(2,1)S(1)}, u32[]{:S(2)}, u32[]{:S(2)}) collective-permute-start(bf16[304,128]{1,0:T(8,128)(2,1)S(1)} %left_sums.1), channel_id=1, source_target_pairs={{4,0},{8,4},{12,8},{16,12},{20,16},{24,20},{28,24},{32,28},{36,32}... | collective-permute-start | bytes 233480 | tf_op jit(solution)/shard_map/ppermute | solution.py:309
  22.1 0.4 %own_sums.1.own_ref = f32[280,128]{1,0:T(8,128)S(1)} custom-call(f32[32,128]{1,0:T(8,128)S(1)} %get-tuple-element.10.taper_ref, f32[528,128]{1,0:T(8,128)S(1)} %get-tuple-element.11.sums_ref), custom_call_target="tpu_custom_call" | custom-call | flops 100000000 | bytes 524288 | tf_op jit(solution)/shard_map/own_sums/pallas_call | solution.py:310
  22.4 0.0 copy-done
  22.4 0.4 %member_means.1 = (f32[16,512]{1,0:T(8,128)S(1)}, bf16[1024,512]{1,0:T(8,128)(2,1)S(1)}) custom-call(bf16[16,64,512]{2,1,0:T(8,128)(2,1)S(1)} %bitcast.7), custom_call_target="tpu_custom_call" | custom-call | flops 100000000 | bytes 524288 | tf_op jit(solution)/shard_map/member_means/pallas_call | solution.py:319
  22.9 0.0 collective-permute-done.before_ref
  22.9 0.6 %collective-permute-done.1.after_ref = bf16[304,128]{1,0:T(8,128)(2,1)S(1)} collective-permute-done((bf16[304,128]{1,0:T(8,128)(2,1)S(1)}, bf16[304,128]{1,0:T(8,128)(2,1)S(1)}, u32[]{:S(2)}, u32[]{:S(2)}) %collective-permute-start.1) | collective-permute-done | bytes 77856 | tf_op jit(solution)/shard_map/ppermute | solution.py:309
  23.5 7.4 %all-gather = bf16[1216,128]{1,0:T(8,128)(2,1)S(1)} all-gather(bf16[304,128]{1,0:T(8,128)(2,1)S(1)} %add_after.1), channel_id=2, replica_groups=mesh['space'=128,'lag'=4] {'lag'}, dimensions={0}, use_global_device_ids=true | all-gather | bytes 389120 | tf_op jit(solution)/shard_map/all_gather | solution.py:344
  30.9 2.8 %transform_apply.1 = bf16[16,64,512]{2,1,0:T(8,128)(2,1)} custom-call(bf16[4,304,128]{2,1,0:T(8,128)(2,1)S(1)} %bitcast.6, f32[16,512]{1,0:T(8,128)S(1)} %get-tuple-element.13.mean_ref, bf16[1024,512]{1,0:T(8,128)(2,1)S(1)} %get-tuple-element.14.anom_ref), custom_call_target="tpu_custom_call" | custom-call | tf_op jit(solution)/shard_map/transform_apply/pallas_call | solution.py:345
  (3 shorter events, 0.1 us)
Async XLA Ops:
  0.0 1.0 %copy-start.1 = (f32[64,2048]{1,0:T(8,128)S(1)}, f32[64,2048]{1,0:T(8,128)}, u32[]{:S(2)}) copy-start(f32[64,2048]{1,0:T(8,128)} %anom_ref.1) | copy-start | bytes 1572868
  0.0 1.0 %copy-start.2 = (f32[2048]{0:T(1024)S(1)}, f32[2048]{0:T(1024)}, u32[]{:S(2)}) copy-start(f32[2048]{0:T(1024)} %param.9) | copy-start | bytes 24580
  0.0 1.0 %copy-start.3 = (f32[2048]{0:T(1024)S(1)}, f32[2048]{0:T(1024)}, u32[]{:S(2)}) copy-start(f32[2048]{0:T(1024)} %param.10) | copy-start | bytes 24580
  0.0 1.0 %copy-start.4 = (s32[2048]{0:T(1024)S(1)}, s32[2048]{0:T(1024)}, u32[]{:S(2)}) copy-start(s32[2048]{0:T(1024)} %param.11) | copy-start | bytes 24580
  0.0 1.0 %copy-start.5 = (f32[32]{0:T(128)S(1)}, f32[32]{0:T(128)}, u32[]{:S(2)}) copy-start(f32[32]{0:T(128)} %taper_ref.1) | copy-start | bytes 388
  0.0 22.4 %copy-start = (bf16[1,16,64,512]{3,2,1,0:T(8,128)(2,1)S(1)}, bf16[1,16,64,512]{3,2,1,0:T(8,128)(2,1)}, u32[]{:S(2)}) copy-start(bf16[1,16,64,512]{3,2,1,0:T(8,128)(2,1)} %param.7) | copy-start | bytes 3145732
  3.2 19.7 %collective-permute-start = (bf16[304,128]{1,0:T(8,128)(2,1)S(1)}, bf16[304,128]{1,0:T(8,128)(2,1)S(1)}, u32[]{:S(2)}, u32[]{:S(2)}) collective-permute-start(bf16[304,128]{1,0:T(8,128)(2,1)S(1)} %get-tuple-element.12), channel_id=1, source_target_pairs={{0,4},{4,8},{8,12},{12,16},{16,20},{20,24},{24,28},{28,32},{32,36}... | collective-permute-start | bytes 233480 | tf_op jit(solution)/shard_map/ppermute | solution.py:299
  7.6 15.9 %collective-permute-start.1 = (bf16[304,128]{1,0:T(8,128)(2,1)S(1)}, bf16[304,128]{1,0:T(8,128)(2,1)S(1)}, u32[]{:S(2)}, u32[]{:S(2)}) collective-permute-start(bf16[304,128]{1,0:T(8,128)(2,1)S(1)} %left_sums.1), channel_id=1, source_target_pairs={{4,0},{8,4},{12,8},{16,12},{20,16},{24,20},{28,24},{32,28},{36,32}... | collective-permute-start | bytes 233480 | tf_op jit(solution)/shard_map/ppermute | solution.py:309

commit v5 on v4

--- a/solution.py
+++ b/solution.py
@@ -96,8 +96,9 @@
 
 def obs_kernel(count_ref, taper_ref, lanes_ref, anom_ref, innov_ref, invv_ref, col_ref, sums_ref, table_ref, right_ref):
     slots = anom_ref.shape[1]
-    for d in range(REACH):
-        table_ref[d : d + 1, :] = jnp.full((1, W), taper_ref[d], F32)
+    square = (REACH, REACH)
+    entries = jnp.where(iota(square, 0) == iota(square, 1), taper_ref[...], 0.0)
+    table_ref[...] = jnp.broadcast_to(jnp.sum(entries, axis=1, keepdims=True), (REACH, W))
     rinv = jnp.where(lanes_ref[0:1, :] < count_ref[0], invv_ref[...], 0.0)
     column = col_ref[...]
     outer, inner = column // Q, column % Q
@@ -290,11 +291,11 @@
     sums, table, right = pl.pallas_call(
         obs_kernel,
         out_shape=[jax.ShapeDtypeStruct((GRAM + 2 * U, W), F32), jax.ShapeDtypeStruct((REACH, W), F32), sent],
-        in_specs=[smem] * 2 + [vmem] * 5,
+        in_specs=[smem] + [vmem] * 6,
         out_specs=[vmem] * 3,
         compiler_params=params,
         name="obs_sums",
-    )(obs_count, taper, lanes, obs_anomaly, innovation[None], inv_variance[None], obs_column[None])
+    )(obs_count, taper[None], lanes, obs_anomaly, innovation[None], inv_variance[None], obs_column[None])
     count = lax.axis_size("space")
     before = lax.ppermute(right, "space", [(i, (i + 1) % count) for i in range(count)])
     left = pl.pallas_call(

time: 33.9 us -> 33.3 us (0.982)
  Pallas kernels: 6.13 us -> 5.57 us
    pallas_call x1, Pallas kernels: 2.1 us -> 1.54 us  [on_device(): pl.pallas_call(obs_kernel, out_shape=[jax.ShapeDtypeStruct((GRAM + 2 * U,...]
where the time goes in v5:
time: 33.3 us; the launch traced here: 33.2 us
  starting transfers between devices  18.5 us (56%)
  blocking collectives  7.36 us (22%)
  Pallas kernels  5.57 us (17%)
  between operations  0.86 us (3%)
  waiting for transfers between devices  0.61 us (2%)
    ppermute x1, starting transfers between devices, on_device(): lax.ppermute(left, 'space', [((i + 1) % count, i) for i in range(count)])  14.5 us
    all_gather x1, blocking collectives, on_device(): parts = lax.all_gather(mixed, 'lag')  7.36 us
    ppermute x1, starting transfers between devices, on_device(): lax.ppermute(right, 'space', [(i, (i + 1) % count) for i in range(count)])  4.03 us
    pallas_call x1, Pallas kernels, on_device(): pl.pallas_call(finish_kernel, out_shape=jax.ShapeDtypeStruct((ncol, K, po...  2.84 us
    pallas_call x1, Pallas kernels, on_device(): pl.pallas_call(obs_kernel, out_shape=[jax.ShapeDtypeStruct((GRAM + 2 * U,...  1.54 us
  transfers between devices with their start and end apart: 2, of which 1 were waited for; matrix products, arithmetic and copies ran while one was open for 0% of the time, Pallas kernels for 3%

profile of v5, /device:TPU:1, one launch (start us, length us, event | category | flops | bytes accessed | tf_op | source)
XLA Modules:
  0.0 33.2 jit_solution(7782682579208131160)
XLA Ops:
  0.0 0.0 copy-start.1
  0.0 0.0 copy-start.2
  0.0 0.0 copy-start.3
  0.0 0.0 copy-start.4
  0.0 0.0 copy-start.5
  0.0 0.0 copy-start
  0.8 0.2 copy-done.1
  1.0 0.0 copy-done.2
  1.0 0.0 copy-done.3
  1.0 0.0 copy-done.4
  1.1 0.0 copy-done.5
  1.1 1.5 %obs_sums.1 = (f32[528,128]{1,0:T(8,128)S(1)}, f32[32,128]{1,0:T(8,128)S(1)}, bf16[304,128]{1,0:T(8,128)(2,1)S(1)}) custom-call(s32[1]{0:T(128)S(6)} %copy.8.count_ref, f32[1,32]{1,0:T(1,128)S(1)} %bitcast.12, s32[8,2048]{1,0:T(8,128)S(1)} %lane_numbers.1.lanes_ref, f32[64,2048]{1,0:T(8,128)S(1)} %copy-done.1, f32[1,2048]{1,0:T(1,128)S(1)} %bitcast.9, ...), custom_call_target="tpu_custom_call" | custom-call | tf_op jit(solution)/shard_map/obs_sums/pallas_call | solution.py:291
  2.6 4.0 %collective-permute-start = (bf16[304,128]{1,0:T(8,128)(2,1)S(1)}, bf16[304,128]{1,0:T(8,128)(2,1)S(1)}, u32[]{:S(2)}, u32[]{:S(2)}) collective-permute-start(bf16[304,128]{1,0:T(8,128)(2,1)S(1)} %get-tuple-element.12), channel_id=1, source_target_pairs={{0,4},{4,8},{8,12},{12,16},{16,20},{20,24},{24,28},{28,32},{32,36}... | collective-permute-start | bytes 233480 | tf_op jit(solution)/shard_map/ppermute | solution.py:300
  6.6 0.4 %left_sums.1 = bf16[304,128]{1,0:T(8,128)(2,1)S(1)} custom-call(f32[32,128]{1,0:T(8,128)S(1)} %get-tuple-element.10.taper_ref, f32[528,128]{1,0:T(8,128)S(1)} %get-tuple-element.11.sums_ref), custom_call_target="tpu_custom_call" | custom-call | flops 100000000 | bytes 524288 | tf_op jit(solution)/shard_map/left_sums/pallas_call | solution.py:301
  7.0 14.5 %collective-permute-start.1 = (bf16[304,128]{1,0:T(8,128)(2,1)S(1)}, bf16[304,128]{1,0:T(8,128)(2,1)S(1)}, u32[]{:S(2)}, u32[]{:S(2)}) collective-permute-start(bf16[304,128]{1,0:T(8,128)(2,1)S(1)} %left_sums.1), channel_id=1, source_target_pairs={{4,0},{8,4},{12,8},{16,12},{20,16},{24,20},{28,24},{32,28},{36,32}... | collective-permute-start | bytes 233480 | tf_op jit(solution)/shard_map/ppermute | solution.py:310
  21.5 0.4 %own_sums.1.own_ref = f32[280,128]{1,0:T(8,128)S(1)} custom-call(f32[32,128]{1,0:T(8,128)S(1)} %get-tuple-element.10.taper_ref, f32[528,128]{1,0:T(8,128)S(1)} %get-tuple-element.11.sums_ref), custom_call_target="tpu_custom_call" | custom-call | flops 100000000 | bytes 524288 | tf_op jit(solution)/shard_map/own_sums/pallas_call | solution.py:311
  21.9 0.0 copy-done
  21.9 0.4 %member_means.1 = (f32[16,512]{1,0:T(8,128)S(1)}, bf16[1024,512]{1,0:T(8,128)(2,1)S(1)}) custom-call(bf16[16,64,512]{2,1,0:T(8,128)(2,1)S(1)} %bitcast.8), custom_call_target="tpu_custom_call" | custom-call | flops 100000000 | bytes 524288 | tf_op jit(solution)/shard_map/member_means/pallas_call | solution.py:320
  22.3 0.0 collective-permute-done.before_ref
  22.3 0.6 %collective-permute-done.1.after_ref = bf16[304,128]{1,0:T(8,128)(2,1)S(1)} collective-permute-done((bf16[304,128]{1,0:T(8,128)(2,1)S(1)}, bf16[304,128]{1,0:T(8,128)(2,1)S(1)}, u32[]{:S(2)}, u32[]{:S(2)}) %collective-permute-start.1) | collective-permute-done | bytes 77856 | tf_op jit(solution)/shard_map/ppermute | solution.py:310
  23.0 7.4 %all-gather = bf16[1216,128]{1,0:T(8,128)(2,1)S(1)} all-gather(bf16[304,128]{1,0:T(8,128)(2,1)S(1)} %add_after.1), channel_id=2, replica_groups=mesh['space'=128,'lag'=4] {'lag'}, dimensions={0}, use_global_device_ids=true | all-gather | bytes 389120 | tf_op jit(solution)/shard_map/all_gather | solution.py:345
  30.3 2.8 %transform_apply.1 = bf16[16,64,512]{2,1,0:T(8,128)(2,1)} custom-call(bf16[4,304,128]{2,1,0:T(8,128)(2,1)S(1)} %bitcast.7, f32[16,512]{1,0:T(8,128)S(1)} %get-tuple-element.13.mean_ref, bf16[1024,512]{1,0:T(8,128)(2,1)S(1)} %get-tuple-element.14.anom_ref), custom_call_target="tpu_custom_call" | custom-call | tf_op jit(solution)/shard_map/transform_apply/pallas_call | solution.py:346
  (3 shorter events, 0.1 us)
Async XLA Ops:
  0.0 1.0 %copy-start.1 = (f32[64,2048]{1,0:T(8,128)S(1)}, f32[64,2048]{1,0:T(8,128)}, u32[]{:S(2)}) copy-start(f32[64,2048]{1,0:T(8,128)} %anom_ref.1) | copy-start | bytes 1572868
  0.0 1.0 %copy-start.2 = (f32[2048]{0:T(1024)S(1)}, f32[2048]{0:T(1024)}, u32[]{:S(2)}) copy-start(f32[2048]{0:T(1024)} %param.9) | copy-start | bytes 24580
  0.0 1.0 %copy-start.3 = (f32[2048]{0:T(1024)S(1)}, f32[2048]{0:T(1024)}, u32[]{:S(2)}) copy-start(f32[2048]{0:T(1024)} %param.10) | copy-start | bytes 24580
  0.0 1.0 %copy-start.4 = (s32[2048]{0:T(1024)S(1)}, s32[2048]{0:T(1024)}, u32[]{:S(2)}) copy-start(s32[2048]{0:T(1024)} %param.11) | copy-start | bytes 24580
  0.0 1.0 %copy-start.5 = (f32[32]{0:T(128)S(1)}, f32[32]{0:T(128)}, u32[]{:S(2)}) copy-start(f32[32]{0:T(128)} %param.13) | copy-start | bytes 388
  0.0 21.8 %copy-start = (bf16[1,16,64,512]{3,2,1,0:T(8,128)(2,1)S(1)}, bf16[1,16,64,512]{3,2,1,0:T(8,128)(2,1)}, u32[]{:S(2)}) copy-start(bf16[1,16,64,512]{3,2,1,0:T(8,128)(2,1)} %param.7) | copy-start | bytes 3145732
  2.6 19.7 %collective-permute-start = (bf16[304,128]{1,0:T(8,128)(2,1)S(1)}, bf16[304,128]{1,0:T(8,128)(2,1)S(1)}, u32[]{:S(2)}, u32[]{:S(2)}) collective-permute-start(bf16[304,128]{1,0:T(8,128)(2,1)S(1)} %get-tuple-element.12), channel_id=1, source_target_pairs={{0,4},{4,8},{8,12},{12,16},{16,20},{20,24},{24,28},{28,32},{32,36}... | collective-permute-start | bytes 233480 | tf_op jit(solution)/shard_map/ppermute | solution.py:300
  7.0 15.9 %collective-permute-start.1 = (bf16[304,128]{1,0:T(8,128)(2,1)S(1)}, bf16[304,128]{1,0:T(8,128)(2,1)S(1)}, u32[]{:S(2)}, u32[]{:S(2)}) collective-permute-start(bf16[304,128]{1,0:T(8,128)(2,1)S(1)} %left_sums.1), channel_id=1, source_target_pairs={{4,0},{8,4},{12,8},{16,12},{20,16},{24,20},{28,24},{32,28},{36,32}... | collective-permute-start | bytes 233480 | tf_op jit(solution)/shard_map/ppermute | solution.py:310

commit v6 on v5

--- a/solution.py
+++ b/solution.py
@@ -5,7 +5,7 @@
 from jax.experimental.pallas import tpu as pltpu
 from jax.sharding import PartitionSpec as P
 
-NS_ITERS = 4
+TWO_STEPS = (2.25, -2.4375, 1.6875, -0.5625, 0.0625)
 K = 64
 REACH = 32
 U = 8
@@ -55,23 +55,24 @@
     def crossed(f):
         return jnp.where(lane < K, at(2 * f + 1), at(2 * f - 1))
 
-    out = [None] * U
-    cross = {f: crossed(f) for f in range(1 - U + U * side, U + U * side)}
+    upper = row <= col
+    half = U // 2
+    straight, cross = {}, {}
+    for f in range(1 - half + U * side, U + U * side):
+        straight[f] = jnp.where(upper, same(f), same(f - half))
+        cross[f] = jnp.where(upper, crossed(f), crossed(f - half))
+    out = [None] * half
     for u in range(U):
         here = sums_ref[K * u : K * (u + 1), :]
         swapped = pltpu.roll(here, K, 1)
-        for v in range(U):
+        for v in range(half):
             f = u - v + U * side
-            term = here * same(f) + swapped * cross[f]
+            term = here * straight[f] + swapped * cross[f]
             out[v] = term if u == 0 else out[v] + term
-    folded = jnp.concatenate([jnp.where(row <= col, out[v], out[v + U // 2]) for v in range(U // 2)], axis=0)
+    folded = jnp.concatenate(out, axis=0)
     sub = iota((U, W), 0)
-    diag = jnp.zeros((U, W), F32)
-    for v in range(U // 2):
-        line = jnp.sum(jnp.where(row == col, out[v + U // 2], 0.0), axis=0, keepdims=True)
-        diag = jnp.where(sub == v, line, diag)
     vectors = []
-    for start in (GRAM, GRAM + U):
+    for start in (GRAM, GRAM + U, GRAM + 2 * U):
         here = sums_ref[start : start + U, :]
         swapped = pltpu.roll(here, K, 1)
         total = jnp.zeros((U, W), F32)
@@ -81,7 +82,7 @@
             total = total + turned * jnp.where(sub >= d, same(f), same(g))
             total = total + also * jnp.where(sub >= d, crossed(f), crossed(g))
         vectors.append(total)
-    return folded, vectors[0], vectors[1], diag
+    return folded, vectors[0], vectors[1], jnp.where(sub < half, pltpu.roll(vectors[2], half, 0), 0.0)
 
 
 def store(out_ref, parts):
@@ -112,7 +113,6 @@
     left.append(jnp.where(row % Q == outer, rows, 0.0))
     lhi, llo = halves(jnp.concatenate(left, axis=0))
     rhi, rlo = halves(jnp.concatenate([jnp.where(inner == b, anom, 0.0) for b in range(Q)], axis=0))
-    mhi, mlo = halves(jnp.where(iota((16, slots), 0) == inner, mean, 0.0))
 
     def dot(a, b):
         return lax.dot_general(a, b, (((1,), (1,)), ((), ())), preferred_element_type=F32)
@@ -120,18 +120,20 @@
     n = Q * K + 16
     both = dot(jnp.concatenate([lhi, llo], axis=0), rhi)
     sums = both[:n] + (both[n:] + dot(lhi, rlo))
-    thi, tlo = lhi[Q * K :], llo[Q * K :]
-    scalars = dot(thi, mhi) + (dot(thi, mlo) + dot(tlo, mhi))
     lane = iota((1, Q * K), 1) // K
     spread = jnp.zeros((8, Q * K), F32)
+    product = left[Q][:8] * mean
     for b in range(Q):
-        spread = jnp.where(lane == b, scalars[:8, b : b + 1], spread)
+        spread = jnp.where(lane == b, jnp.sum(jnp.where(inner == b, product, 0.0), axis=1, keepdims=True), spread)
     factor = jnp.where(iota((8, 1), 0) < Q, 1.0, 0.5)
     vectors = sums[Q * K : Q * K + 8] + spread * factor
+    on = iota((K, W), 0) == iota((K, W), 1) % K
     for a in range(Q):
         for i in range(2):
             u = 2 * a + i
-            sums_ref[K * u : K * (u + 1), :] = sums[K * a : K * (a + 1), W * i : W * (i + 1)]
+            here = sums[K * a : K * (a + 1), W * i : W * (i + 1)]
+            sums_ref[K * u : K * (u + 1), :] = here
+            sums_ref[GRAM + 2 * U + u : GRAM + 2 * U + u + 1, :] = jnp.sum(jnp.where(on, here, 0.0), axis=0, keepdims=True)
             sums_ref[GRAM + u : GRAM + u + 1, :] = vectors[a : a + 1, W * i : W * (i + 1)]
             sums_ref[GRAM + U + u : GRAM + U + u + 1, :] = vectors[Q + a : Q + a + 1, W * i : W * (i + 1)]
     store(right_ref, mix(sums_ref, table_ref, -1))
@@ -241,16 +243,16 @@
     scale = [scale[g : g + 1] for g in range(groups)]
     square = [times([a], a)[0] for a in amat]
     inverse = [1.0 / s for s in scale]
-    zval = [1.5 * eye - (0.5 * i) * a for a, i in zip(amat, inverse)]
-    yval = [(1.5 * i) * a - (0.5 * i * i) * q for a, i, q in zip(amat, inverse, square)]
-    for step in range(1, NS_ITERS):
-        prod = [times([z], y)[0] for z, y in zip(zval, yval)]
-        mval = [1.5 * eye - 0.5 * p for p in prod]
-        if step < NS_ITERS - 1:
-            both = [times([y, z], m) for y, z, m in zip(yval, zval, mval)]
-            yval, zval = [b[0] for b in both], [b[1] for b in both]
-        else:
-            zval = [times([z], m)[0] for z, m in zip(zval, mval)]
+    one, two, three, four, five = TWO_STEPS
+    x1 = [i * a for a, i in zip(amat, inverse)]
+    x2 = [(i * i) * q for q, i in zip(square, inverse)]
+    more = [times([p, q], q) for p, q in zip(x1, x2)]
+    zval = [one * eye + two * p + three * q + (four * m[0] + five * m[1]) for p, q, m in zip(x1, x2, more)]
+    more = [times([p, z], z) for p, z in zip(x1, zval)]
+    more = [times([z, m[1]], m[0]) for z, m in zip(zval, more)]
+    third = [times([m[0], m[1]], m[0]) for m in more]
+    last = [times([four * m[1] + five * t[1]], t[0])[0] for m, t in zip(more, third)]
+    zval = [one * z + two * m[1] + three * t[1] + y for z, m, t, y in zip(zval, more, third, last)]
     weights = []
     for g in range(groups):
         inner = lane_sums(zval[g] * bvec[g])
@@ -290,7 +292,7 @@
     )()
     sums, table, right = pl.pallas_call(
         obs_kernel,
-        out_shape=[jax.ShapeDtypeStruct((GRAM + 2 * U, W), F32), jax.ShapeDtypeStruct((REACH, W), F32), sent],
+        out_shape=[jax.ShapeDtypeStruct((GRAM + 3 * U, W), F32), jax.ShapeDtypeStruct((REACH, W), F32), sent],
         in_specs=[smem] + [vmem] * 6,
         out_specs=[vmem] * 3,
         compiler_params=params,

time: 33.3 us -> 32.9 us (0.988)
  Pallas kernels: 5.57 us -> 5 us
where the time goes in v6:
time: 32.9 us; the launch traced here: 32.7 us
  starting transfers between devices  18.5 us (56%)
  blocking collectives  7.36 us (22%)
  Pallas kernels  5 us (15%)
  between operations  0.86 us (3%)
  waiting for transfers between devices  0.73 us (2%)
    ppermute x1, starting transfers between devices, on_device(): lax.ppermute(left, 'space', [((i + 1) % count, i) for i in range(count)])  14.5 us
    all_gather x1, blocking collectives, on_device(): parts = lax.all_gather(mixed, 'lag')  7.36 us
    ppermute x1, starting transfers between devices, on_device(): lax.ppermute(right, 'space', [(i, (i + 1) % count) for i in range(count)])  4.04 us
    pallas_call x1, Pallas kernels, on_device(): pl.pallas_call(finish_kernel, out_shape=jax.ShapeDtypeStruct((ncol, K, po...  2.78 us
    pallas_call x1, Pallas kernels, on_device(): pl.pallas_call(obs_kernel, out_shape=[jax.ShapeDtypeStruct((GRAM + 3 * U,...  1.28 us
    ppermute x1, waiting for transfers between devices, on_device(): lax.ppermute(left, 'space', [((i + 1) % count, i) for i in range(count)])  0.73 us
  transfers between devices with their start and end apart: 2, of which 1 were waited for; matrix products, arithmetic and copies ran while one was open for 0% of the time, Pallas kernels for 3%

profile of v6, /device:TPU:1, one launch (start us, length us, event | category | flops | bytes accessed | tf_op | source)
XLA Modules:
  0.0 32.7 jit_solution(10581688649297022861)
XLA Ops:
  0.0 0.0 copy-start.1
  0.0 0.0 copy-start.2
  0.0 0.0 copy-start.3
  0.0 0.0 copy-start.4
  0.0 0.0 copy-start.5
  0.0 0.0 copy-start
  0.8 0.2 copy-done.1
  1.0 0.0 copy-done.2
  1.0 0.0 copy-done.3
  1.0 0.0 copy-done.4
  1.1 0.0 copy-done.5
  1.1 1.3 %obs_sums.1 = (f32[536,128]{1,0:T(8,128)S(1)}, f32[32,128]{1,0:T(8,128)S(1)}, bf16[304,128]{1,0:T(8,128)(2,1)S(1)}) custom-call(s32[1]{0:T(128)S(6)} %copy.8.count_ref, f32[1,32]{1,0:T(1,128)S(1)} %bitcast.12, s32[8,2048]{1,0:T(8,128)S(1)} %lane_numbers.1.lanes_ref, f32[64,2048]{1,0:T(8,128)S(1)} %copy-done.1, f32[1,2048]{1,0:T(1,128)S(1)} %bitcast.9, ...), custom_call_target="tpu_custom_call" | custom-call | tf_op jit(solution)/shard_map/obs_sums/pallas_call | solution.py:293
  2.3 4.0 %collective-permute-start = (bf16[304,128]{1,0:T(8,128)(2,1)S(1)}, bf16[304,128]{1,0:T(8,128)(2,1)S(1)}, u32[]{:S(2)}, u32[]{:S(2)}) collective-permute-start(bf16[304,128]{1,0:T(8,128)(2,1)S(1)} %get-tuple-element.12), channel_id=1, source_target_pairs={{0,4},{4,8},{8,12},{12,16},{16,20},{20,24},{24,28},{28,32},{32,36}... | collective-permute-start | bytes 233480 | tf_op jit(solution)/shard_map/ppermute | solution.py:302
  6.4 0.2 left_sums.1
  6.6 14.5 %collective-permute-start.1 = (bf16[304,128]{1,0:T(8,128)(2,1)S(1)}, bf16[304,128]{1,0:T(8,128)(2,1)S(1)}, u32[]{:S(2)}, u32[]{:S(2)}) collective-permute-start(bf16[304,128]{1,0:T(8,128)(2,1)S(1)} %left_sums.1), channel_id=1, source_target_pairs={{4,0},{8,4},{12,8},{16,12},{20,16},{24,20},{28,24},{32,28},{36,32}... | collective-permute-start | bytes 233480 | tf_op jit(solution)/shard_map/ppermute | solution.py:312
  21.1 0.2 own_sums.1.own_ref
  21.4 0.0 copy-done
  21.4 0.4 %member_means.1 = (f32[16,512]{1,0:T(8,128)S(1)}, bf16[1024,512]{1,0:T(8,128)(2,1)S(1)}) custom-call(bf16[16,64,512]{2,1,0:T(8,128)(2,1)S(1)} %bitcast.8), custom_call_target="tpu_custom_call" | custom-call | flops 100000000 | bytes 524288 | tf_op jit(solution)/shard_map/member_means/pallas_call | solution.py:322
  21.8 0.0 collective-permute-done.before_ref
  21.8 0.7 %collective-permute-done.1.after_ref = bf16[304,128]{1,0:T(8,128)(2,1)S(1)} collective-permute-done((bf16[304,128]{1,0:T(8,128)(2,1)S(1)}, bf16[304,128]{1,0:T(8,128)(2,1)S(1)}, u32[]{:S(2)}, u32[]{:S(2)}) %collective-permute-start.1) | collective-permute-done | bytes 77856 | tf_op jit(solution)/shard_map/ppermute | solution.py:312
  22.6 7.4 %all-gather = bf16[1216,128]{1,0:T(8,128)(2,1)S(1)} all-gather(bf16[304,128]{1,0:T(8,128)(2,1)S(1)} %add_after.1), channel_id=2, replica_groups=mesh['space'=128,'lag'=4] {'lag'}, dimensions={0}, use_global_device_ids=true | all-gather | bytes 389120 | tf_op jit(solution)/shard_map/all_gather | solution.py:347
  29.9 2.8 %transform_apply.1 = bf16[16,64,512]{2,1,0:T(8,128)(2,1)} custom-call(bf16[4,304,128]{2,1,0:T(8,128)(2,1)S(1)} %bitcast.7, f32[16,512]{1,0:T(8,128)S(1)} %get-tuple-element.13.mean_ref, bf16[1024,512]{1,0:T(8,128)(2,1)S(1)} %get-tuple-element.14.anom_ref), custom_call_target="tpu_custom_call" | custom-call | tf_op jit(solution)/shard_map/transform_apply/pallas_call | solution.py:348
  (3 shorter events, 0.1 us)
Async XLA Ops:
  0.0 1.0 %copy-start.1 = (f32[64,2048]{1,0:T(8,128)S(1)}, f32[64,2048]{1,0:T(8,128)}, u32[]{:S(2)}) copy-start(f32[64,2048]{1,0:T(8,128)} %anom_ref.1) | copy-start | bytes 1572868
  0.0 1.0 %copy-start.2 = (f32[2048]{0:T(1024)S(1)}, f32[2048]{0:T(1024)}, u32[]{:S(2)}) copy-start(f32[2048]{0:T(1024)} %param.9) | copy-start | bytes 24580
  0.0 1.0 %copy-start.3 = (f32[2048]{0:T(1024)S(1)}, f32[2048]{0:T(1024)}, u32[]{:S(2)}) copy-start(f32[2048]{0:T(1024)} %param.10) | copy-start | bytes 24580
  0.0 1.0 %copy-start.4 = (s32[2048]{0:T(1024)S(1)}, s32[2048]{0:T(1024)}, u32[]{:S(2)}) copy-start(s32[2048]{0:T(1024)} %param.11) | copy-start | bytes 24580
  0.0 1.0 %copy-start.5 = (f32[32]{0:T(128)S(1)}, f32[32]{0:T(128)}, u32[]{:S(2)}) copy-start(f32[32]{0:T(128)} %param.13) | copy-start | bytes 388
  0.0 21.3 %copy-start = (bf16[1,16,64,512]{3,2,1,0:T(8,128)(2,1)S(1)}, bf16[1,16,64,512]{3,2,1,0:T(8,128)(2,1)}, u32[]{:S(2)}) copy-start(bf16[1,16,64,512]{3,2,1,0:T(8,128)(2,1)} %param.7) | copy-start | bytes 3145732
  2.3 19.4 %collective-permute-start = (bf16[304,128]{1,0:T(8,128)(2,1)S(1)}, bf16[304,128]{1,0:T(8,128)(2,1)S(1)}, u32[]{:S(2)}, u32[]{:S(2)}) collective-permute-start(bf16[304,128]{1,0:T(8,128)(2,1)S(1)} %get-tuple-element.12), channel_id=1, source_target_pairs={{0,4},{4,8},{8,12},{12,16},{16,20},{20,24},{24,28},{28,32},{32,36}... | collective-permute-start | bytes 233480 | tf_op jit(solution)/shard_map/ppermute | solution.py:302
  6.6 15.9 %collective-permute-start.1 = (bf16[304,128]{1,0:T(8,128)(2,1)S(1)}, bf16[304,128]{1,0:T(8,128)(2,1)S(1)}, u32[]{:S(2)}, u32[]{:S(2)}) collective-permute-start(bf16[304,128]{1,0:T(8,128)(2,1)S(1)} %left_sums.1), channel_id=1, source_target_pairs={{4,0},{8,4},{12,8},{16,12},{20,16},{24,20},{28,24},{32,28},{36,32}... | collective-permute-start | bytes 233480 | tf_op jit(solution)/shard_map/ppermute | solution.py:312

commit v7 on v6

--- a/solution.py
+++ b/solution.py
@@ -13,7 +13,7 @@
 Q = 4
 GRAM = U * K
 HALF = GRAM // 2
-SENT = HALF + 48
+SENT = HALF + 40
 F32 = jnp.float32
 BF16 = jnp.bfloat16
 VMEM = pltpu.VMEM
@@ -31,14 +31,14 @@
 def encode(folded, bvec, mvec, diag):
     bhi, blo = halves(bvec)
     mhi, mlo = halves(mvec)
-    rest = [x.astype(F32) for x in (bhi, blo, mhi, mlo)] + [diag, jnp.zeros_like(diag)]
-    return folded.astype(BF16), jnp.concatenate(rest, axis=0).astype(BF16)
-
-
-def decode(ref, at=()):
-    whole = ref[at + (slice(0, HALF),)].astype(F32)
-    rest = ref[at + (slice(HALF, SENT),)].astype(F32)
-    return whole, rest[0:8] + rest[8:16], rest[16:24] + rest[24:32], rest[32:40]
+    rest = [x.astype(F32) for x in (bhi, blo, mhi, mlo)]
+    return jnp.concatenate([folded, *rest, diag], axis=0).astype(BF16)
+
+
+def decode(sent):
+    whole = sent.astype(F32)
+    bhi, blo, mhi, mlo, diag = (whole[HALF + 8 * i : HALF + 8 * (i + 1)] for i in range(5))
+    return whole[:HALF], bhi + blo, mhi + mlo, diag
 
 
 def mix(sums_ref, taper_ref, side):
@@ -86,9 +86,7 @@
 
 
 def store(out_ref, parts):
-    folded, rest = encode(*parts)
-    out_ref[0:HALF, :] = folded
-    out_ref[HALF:SENT, :] = rest
+    out_ref[...] = encode(*parts)
 
 
 def lanes_kernel(out_ref):
@@ -160,11 +158,11 @@
 
 
 def before_kernel(own_ref, before_ref, out_ref):
-    put(out_ref, [x + y for x, y in zip(get(own_ref), decode(before_ref))])
+    put(out_ref, [x + y for x, y in zip(get(own_ref), decode(before_ref[...]))])
 
 
 def after_kernel(own_ref, after_ref, out_ref):
-    store(out_ref, [x + y for x, y in zip(get(own_ref), decode(after_ref))])
+    store(out_ref, [x + y for x, y in zip(get(own_ref), decode(after_ref[...]))])
 
 
 def members_kernel(ens_ref, mean_ref, anom_ref):
@@ -209,9 +207,9 @@
             out = jnp.where(lane == cc, jnp.sum(jnp.where(lane == cc, x, 0.0), axis=1, keepdims=True), out)
         return out
 
-    folded, bvec, mvec, diag = decode(parts_ref, (0,))
+    folded, bvec, mvec, diag = decode(parts_ref[0])
     for lag in range(1, parts_ref.shape[0]):
-        more = decode(parts_ref, (lag,))
+        more = decode(parts_ref[lag])
         folded, bvec, mvec, diag = folded + more[0], bvec + more[1], mvec + more[2], diag + more[3]
     units = [None] * U
     for v in range(U // 2):

time: 32.9 us -> 32.8 us (level)
  no operation moved by 1% of the time
where the time goes in v7:
time: 32.8 us; the launch traced here: 32.6 us
  starting transfers between devices  18.5 us (56%)
  blocking collectives  7.32 us (22%)
  Pallas kernels  5 us (15%)
  between operations  0.86 us (3%)
  waiting for transfers between devices  0.71 us (2%)
    ppermute x1, starting transfers between devices, on_device(): lax.ppermute(left, 'space', [((i + 1) % count, i) for i in range(count)])  14.5 us
    all_gather x1, blocking collectives, on_device(): parts = lax.all_gather(mixed, 'lag')  7.32 us
    ppermute x1, starting transfers between devices, on_device(): lax.ppermute(right, 'space', [(i, (i + 1) % count) for i in range(count)])  4.04 us
    pallas_call x1, Pallas kernels, on_device(): pl.pallas_call(finish_kernel, out_shape=jax.ShapeDtypeStruct((ncol, K, po...  2.77 us
    pallas_call x1, Pallas kernels, on_device(): pl.pallas_call(obs_kernel, out_shape=[jax.ShapeDtypeStruct((GRAM + 3 * U,...  1.28 us
    ppermute x1, waiting for transfers between devices, on_device(): lax.ppermute(left, 'space', [((i + 1) % count, i) for i in range(count)])  0.71 us
  transfers between devices with their start and end apart: 2, of which 1 were waited for; matrix products, arithmetic and copies ran while one was open for 0% of the time, Pallas kernels for 3%

profile of v7, /device:TPU:1, one launch (start us, length us, event | category | flops | bytes accessed | tf_op | source)
XLA Modules:
  0.0 32.6 jit_solution(574140671521517894)
XLA Ops:
  0.0 0.0 copy-start.1
  0.0 0.0 copy-start.2
  0.0 0.0 copy-start.3
  0.0 0.0 copy-start.4
  0.0 0.0 copy-start.5
  0.0 0.0 copy-start
  0.8 0.2 copy-done.1
  1.0 0.0 copy-done.2
  1.0 0.0 copy-done.3
  1.0 0.0 copy-done.4
  1.1 0.0 copy-done.5
  1.1 1.3 %obs_sums.1 = (f32[536,128]{1,0:T(8,128)S(1)}, f32[32,128]{1,0:T(8,128)S(1)}, bf16[296,128]{1,0:T(8,128)(2,1)S(1)}) custom-call(s32[1]{0:T(128)S(6)} %copy.8.count_ref, f32[1,32]{1,0:T(1,128)S(1)} %bitcast.12, s32[8,2048]{1,0:T(8,128)S(1)} %lane_numbers.1.lanes_ref, f32[64,2048]{1,0:T(8,128)S(1)} %copy-done.1, f32[1,2048]{1,0:T(1,128)S(1)} %bitcast.9, ...), custom_call_target="tpu_custom_call" | custom-call | tf_op jit(solution)/shard_map/obs_sums/pallas_call | solution.py:291
  2.3 4.0 %collective-permute-start = (bf16[296,128]{1,0:T(8,128)(2,1)S(1)}, bf16[296,128]{1,0:T(8,128)(2,1)S(1)}, u32[]{:S(2)}, u32[]{:S(2)}) collective-permute-start(bf16[296,128]{1,0:T(8,128)(2,1)S(1)} %get-tuple-element.12), channel_id=1, source_target_pairs={{0,4},{4,8},{8,12},{12,16},{16,20},{20,24},{24,28},{28,32},{32,36}... | collective-permute-start | bytes 227336 | tf_op jit(solution)/shard_map/ppermute | solution.py:300
  6.4 0.2 left_sums.1
  6.6 14.5 %collective-permute-start.1 = (bf16[296,128]{1,0:T(8,128)(2,1)S(1)}, bf16[296,128]{1,0:T(8,128)(2,1)S(1)}, u32[]{:S(2)}, u32[]{:S(2)}) collective-permute-start(bf16[296,128]{1,0:T(8,128)(2,1)S(1)} %left_sums.1), channel_id=1, source_target_pairs={{4,0},{8,4},{12,8},{16,12},{20,16},{24,20},{28,24},{32,28},{36,32}... | collective-permute-start | bytes 227336 | tf_op jit(solution)/shard_map/ppermute | solution.py:310
  21.1 0.2 own_sums.1.own_ref
  21.4 0.0 copy-done
  21.4 0.4 %member_means.1 = (f32[16,512]{1,0:T(8,128)S(1)}, bf16[1024,512]{1,0:T(8,128)(2,1)S(1)}) custom-call(bf16[16,64,512]{2,1,0:T(8,128)(2,1)S(1)} %bitcast.8), custom_call_target="tpu_custom_call" | custom-call | flops 100000000 | bytes 524288 | tf_op jit(solution)/shard_map/member_means/pallas_call | solution.py:320
  21.8 0.0 collective-permute-done.before_ref
  21.8 0.7 %collective-permute-done.1.after_ref = bf16[296,128]{1,0:T(8,128)(2,1)S(1)} collective-permute-done((bf16[296,128]{1,0:T(8,128)(2,1)S(1)}, bf16[296,128]{1,0:T(8,128)(2,1)S(1)}, u32[]{:S(2)}, u32[]{:S(2)}) %collective-permute-start.1) | collective-permute-done | bytes 75808 | tf_op jit(solution)/shard_map/ppermute | solution.py:310
  22.6 7.3 %all-gather = bf16[1184,128]{1,0:T(8,128)(2,1)S(1)} all-gather(bf16[296,128]{1,0:T(8,128)(2,1)S(1)} %add_after.1), channel_id=2, replica_groups=mesh['space'=128,'lag'=4] {'lag'}, dimensions={0}, use_global_device_ids=true | all-gather | bytes 378880 | tf_op jit(solution)/shard_map/all_gather | solution.py:345
  29.9 2.8 %transform_apply.1 = bf16[16,64,512]{2,1,0:T(8,128)(2,1)} custom-call(bf16[4,296,128]{2,1,0:T(8,128)(2,1)S(1)} %bitcast.7, f32[16,512]{1,0:T(8,128)S(1)} %get-tuple-element.13.mean_ref, bf16[1024,512]{1,0:T(8,128)(2,1)S(1)} %get-tuple-element.14.anom_ref), custom_call_target="tpu_custom_call" | custom-call | tf_op jit(solution)/shard_map/transform_apply/pallas_call | solution.py:346
  (3 shorter events, 0.1 us)
Async XLA Ops:
  0.0 1.0 %copy-start.1 = (f32[64,2048]{1,0:T(8,128)S(1)}, f32[64,2048]{1,0:T(8,128)}, u32[]{:S(2)}) copy-start(f32[64,2048]{1,0:T(8,128)} %anom_ref.1) | copy-start | bytes 1572868
  0.0 1.0 %copy-start.2 = (f32[2048]{0:T(1024)S(1)}, f32[2048]{0:T(1024)}, u32[]{:S(2)}) copy-start(f32[2048]{0:T(1024)} %param.9) | copy-start | bytes 24580
  0.0 1.0 %copy-start.3 = (f32[2048]{0:T(1024)S(1)}, f32[2048]{0:T(1024)}, u32[]{:S(2)}) copy-start(f32[2048]{0:T(1024)} %param.10) | copy-start | bytes 24580
  0.0 1.0 %copy-start.4 = (s32[2048]{0:T(1024)S(1)}, s32[2048]{0:T(1024)}, u32[]{:S(2)}) copy-start(s32[2048]{0:T(1024)} %param.11) | copy-start | bytes 24580
  0.0 1.0 %copy-start.5 = (f32[32]{0:T(128)S(1)}, f32[32]{0:T(128)}, u32[]{:S(2)}) copy-start(f32[32]{0:T(128)} %param.13) | copy-start | bytes 388
  0.0 21.3 %copy-start = (bf16[1,16,64,512]{3,2,1,0:T(8,128)(2,1)S(1)}, bf16[1,16,64,512]{3,2,1,0:T(8,128)(2,1)}, u32[]{:S(2)}) copy-start(bf16[1,16,64,512]{3,2,1,0:T(8,128)(2,1)} %param.7) | copy-start | bytes 3145732
  2.3 19.4 %collective-permute-start = (bf16[296,128]{1,0:T(8,128)(2,1)S(1)}, bf16[296,128]{1,0:T(8,128)(2,1)S(1)}, u32[]{:S(2)}, u32[]{:S(2)}) collective-permute-start(bf16[296,128]{1,0:T(8,128)(2,1)S(1)} %get-tuple-element.12), channel_id=1, source_target_pairs={{0,4},{4,8},{8,12},{12,16},{16,20},{20,24},{24,28},{28,32},{32,36}... | collective-permute-start | bytes 227336 | tf_op jit(solution)/shard_map/ppermute | solution.py:300
  6.6 15.9 %collective-permute-start.1 = (bf16[296,128]{1,0:T(8,128)(2,1)S(1)}, bf16[296,128]{1,0:T(8,128)(2,1)S(1)}, u32[]{:S(2)}, u32[]{:S(2)}) collective-permute-start(bf16[296,128]{1,0:T(8,128)(2,1)S(1)} %left_sums.1), channel_id=1, source_target_pairs={{4,0},{8,4},{12,8},{16,12},{20,16},{24,20},{28,24},{32,28},{36,32}... | collective-permute-start | bytes 227336 | tf_op jit(solution)/shard_map/ppermute | solution.py:310

commit v8 on v7

--- a/solution.py
+++ b/solution.py
@@ -184,8 +184,8 @@
     left_half = iota((K, W), 1) < K
 
     def spread(x):
-        tall = jnp.concatenate([x] * n, axis=0)
-        return jnp.where(diagonal, tall, jnp.zeros_like(tall))
+        zero = jnp.zeros_like(x)
+        return jnp.concatenate([jnp.where(left_half, x, zero), jnp.where(left_half, zero, x)], axis=0)
 
     def dot(a, b):
         return jnp.dot(a, b, preferred_element_type=F32)

time: 32.8 us -> 32.8 us (level)
  no operation moved by 1% of the time
where the time goes in v8:
time: 32.8 us; the launch traced here: 32.6 us
  starting transfers between devices  18.5 us (56%)
  blocking collectives  7.32 us (22%)
  Pallas kernels  4.98 us (15%)
  between operations  0.86 us (3%)
  waiting for transfers between devices  0.71 us (2%)
    ppermute x1, starting transfers between devices, on_device(): lax.ppermute(left, 'space', [((i + 1) % count, i) for i in range(count)])  14.5 us
    all_gather x1, blocking collectives, on_device(): parts = lax.all_gather(mixed, 'lag')  7.32 us
    ppermute x1, starting transfers between devices, on_device(): lax.ppermute(right, 'space', [(i, (i + 1) % count) for i in range(count)])  4.04 us
    pallas_call x1, Pallas kernels, on_device(): pl.pallas_call(finish_kernel, out_shape=jax.ShapeDtypeStruct((ncol, K, po...  2.75 us
    pallas_call x1, Pallas kernels, on_device(): pl.pallas_call(obs_kernel, out_shape=[jax.ShapeDtypeStruct((GRAM + 3 * U,...  1.28 us
    ppermute x1, waiting for transfers between devices, on_device(): lax.ppermute(left, 'space', [((i + 1) % count, i) for i in range(count)])  0.71 us
  transfers between devices with their start and end apart: 2, of which 1 were waited for; matrix products, arithmetic and copies ran while one was open for 0% of the time, Pallas kernels for 3%

profile of v8, /device:TPU:1, one launch (start us, length us, event | category | flops | bytes accessed | tf_op | source)
XLA Modules:
  0.0 32.6 jit_solution(13785571569972627703)
XLA Ops:
  0.0 0.0 copy-start.1
  0.0 0.0 copy-start.2
  0.0 0.0 copy-start.3
  0.0 0.0 copy-start.4
  0.0 0.0 copy-start.5
  0.0 0.0 copy-start
  0.8 0.2 copy-done.1
  1.0 0.0 copy-done.2
  1.0 0.0 copy-done.3
  1.0 0.0 copy-done.4
  1.1 0.0 copy-done.5
  1.1 1.3 %obs_sums.1 = (f32[536,128]{1,0:T(8,128)S(1)}, f32[32,128]{1,0:T(8,128)S(1)}, bf16[296,128]{1,0:T(8,128)(2,1)S(1)}) custom-call(s32[1]{0:T(128)S(6)} %copy.8.count_ref, f32[1,32]{1,0:T(1,128)S(1)} %bitcast.12, s32[8,2048]{1,0:T(8,128)S(1)} %lane_numbers.1.lanes_ref, f32[64,2048]{1,0:T(8,128)S(1)} %copy-done.1, f32[1,2048]{1,0:T(1,128)S(1)} %bitcast.9, ...), custom_call_target="tpu_custom_call" | custom-call | tf_op jit(solution)/shard_map/obs_sums/pallas_call | solution.py:291
  2.3 4.0 %collective-permute-start = (bf16[296,128]{1,0:T(8,128)(2,1)S(1)}, bf16[296,128]{1,0:T(8,128)(2,1)S(1)}, u32[]{:S(2)}, u32[]{:S(2)}) collective-permute-start(bf16[296,128]{1,0:T(8,128)(2,1)S(1)} %get-tuple-element.12), channel_id=1, source_target_pairs={{0,4},{4,8},{8,12},{12,16},{16,20},{20,24},{24,28},{28,32},{32,36}... | collective-permute-start | bytes 227336 | tf_op jit(solution)/shard_map/ppermute | solution.py:300
  6.4 0.2 left_sums.1
  6.6 14.5 %collective-permute-start.1 = (bf16[296,128]{1,0:T(8,128)(2,1)S(1)}, bf16[296,128]{1,0:T(8,128)(2,1)S(1)}, u32[]{:S(2)}, u32[]{:S(2)}) collective-permute-start(bf16[296,128]{1,0:T(8,128)(2,1)S(1)} %left_sums.1), channel_id=1, source_target_pairs={{4,0},{8,4},{12,8},{16,12},{20,16},{24,20},{28,24},{32,28},{36,32}... | collective-permute-start | bytes 227336 | tf_op jit(solution)/shard_map/ppermute | solution.py:310
  21.1 0.2 own_sums.1.own_ref
  21.4 0.0 copy-done
  21.4 0.4 %member_means.1 = (f32[16,512]{1,0:T(8,128)S(1)}, bf16[1024,512]{1,0:T(8,128)(2,1)S(1)}) custom-call(bf16[16,64,512]{2,1,0:T(8,128)(2,1)S(1)} %bitcast.8), custom_call_target="tpu_custom_call" | custom-call | flops 100000000 | bytes 524288 | tf_op jit(solution)/shard_map/member_means/pallas_call | solution.py:320
  21.8 0.0 collective-permute-done.before_ref
  21.8 0.7 %collective-permute-done.1.after_ref = bf16[296,128]{1,0:T(8,128)(2,1)S(1)} collective-permute-done((bf16[296,128]{1,0:T(8,128)(2,1)S(1)}, bf16[296,128]{1,0:T(8,128)(2,1)S(1)}, u32[]{:S(2)}, u32[]{:S(2)}) %collective-permute-start.1) | collective-permute-done | bytes 75808 | tf_op jit(solution)/shard_map/ppermute | solution.py:310
  22.6 7.3 %all-gather = bf16[1184,128]{1,0:T(8,128)(2,1)S(1)} all-gather(bf16[296,128]{1,0:T(8,128)(2,1)S(1)} %add_after.1), channel_id=2, replica_groups=mesh['space'=128,'lag'=4] {'lag'}, dimensions={0}, use_global_device_ids=true | all-gather | bytes 378880 | tf_op jit(solution)/shard_map/all_gather | solution.py:345
  29.9 2.8 %transform_apply.1 = bf16[16,64,512]{2,1,0:T(8,128)(2,1)} custom-call(bf16[4,296,128]{2,1,0:T(8,128)(2,1)S(1)} %bitcast.7, f32[16,512]{1,0:T(8,128)S(1)} %get-tuple-element.13.mean_ref, bf16[1024,512]{1,0:T(8,128)(2,1)S(1)} %get-tuple-element.14.anom_ref), custom_call_target="tpu_custom_call" | custom-call | tf_op jit(solution)/shard_map/transform_apply/pallas_call | solution.py:346
  (3 shorter events, 0.1 us)
Async XLA Ops:
  0.0 1.0 %copy-start.1 = (f32[64,2048]{1,0:T(8,128)S(1)}, f32[64,2048]{1,0:T(8,128)}, u32[]{:S(2)}) copy-start(f32[64,2048]{1,0:T(8,128)} %anom_ref.1) | copy-start | bytes 1572868
  0.0 1.0 %copy-start.2 = (f32[2048]{0:T(1024)S(1)}, f32[2048]{0:T(1024)}, u32[]{:S(2)}) copy-start(f32[2048]{0:T(1024)} %param.9) | copy-start | bytes 24580
  0.0 1.0 %copy-start.3 = (f32[2048]{0:T(1024)S(1)}, f32[2048]{0:T(1024)}, u32[]{:S(2)}) copy-start(f32[2048]{0:T(1024)} %param.10) | copy-start | bytes 24580
  0.0 1.0 %copy-start.4 = (s32[2048]{0:T(1024)S(1)}, s32[2048]{0:T(1024)}, u32[]{:S(2)}) copy-start(s32[2048]{0:T(1024)} %param.11) | copy-start | bytes 24580
  0.0 1.0 %copy-start.5 = (f32[32]{0:T(128)S(1)}, f32[32]{0:T(128)}, u32[]{:S(2)}) copy-start(f32[32]{0:T(128)} %param.13) | copy-start | bytes 388
  0.0 21.3 %copy-start = (bf16[1,16,64,512]{3,2,1,0:T(8,128)(2,1)S(1)}, bf16[1,16,64,512]{3,2,1,0:T(8,128)(2,1)}, u32[]{:S(2)}) copy-start(bf16[1,16,64,512]{3,2,1,0:T(8,128)(2,1)} %param.7) | copy-start | bytes 3145732
  2.3 19.4 %collective-permute-start = (bf16[296,128]{1,0:T(8,128)(2,1)S(1)}, bf16[296,128]{1,0:T(8,128)(2,1)S(1)}, u32[]{:S(2)}, u32[]{:S(2)}) collective-permute-start(bf16[296,128]{1,0:T(8,128)(2,1)S(1)} %get-tuple-element.12), channel_id=1, source_target_pairs={{0,4},{4,8},{8,12},{12,16},{16,20},{20,24},{24,28},{28,32},{32,36}... | collective-permute-start | bytes 227336 | tf_op jit(solution)/shard_map/ppermute | solution.py:300
  6.6 15.9 %collective-permute-start.1 = (bf16[296,128]{1,0:T(8,128)(2,1)S(1)}, bf16[296,128]{1,0:T(8,128)(2,1)S(1)}, u32[]{:S(2)}, u32[]{:S(2)}) collective-permute-start(bf16[296,128]{1,0:T(8,128)(2,1)S(1)} %left_sums.1), channel_id=1, source_target_pairs={{4,0},{8,4},{12,8},{16,12},{20,16},{24,20},{28,24},{32,28},{36,32}... | collective-permute-start | bytes 227336 | tf_op jit(solution)/shard_map/ppermute | solution.py:310
